TPU v7x, 256 devices: a whole 4x4x8 slice. The times are simulated.
256 devices in a mesh: section: 16 (over z, core), dp: 8 (over y_lo, x), tensor: 2 (over y_hi).
Axes of the slice: x: 4, y: 4 (y_hi: 2, y_lo: 2; y = y_hi * 2 + y_lo), z: 8, core: 2. Of those that a mesh axis runs over, the one named last changes fastest.
Arguments:
- embeddings: bfloat16 [2048, 6144], P('dp', 'tensor'), may hold values from -110 to 110
- section_outputs: bfloat16 [16, 2048, 6144], P('section', 'dp', 'tensor'), may hold values from -110 to 110
- norm_gain: float32 [16, 6144], P('section', 'tensor'), may hold values from 0.1 to 1.9
- input_grads: bfloat16 [16, 2048, 6144], P('section', 'dp', 'tensor'), may hold values from -16 to 16
- loss_grads: bfloat16 [2048, 6144], P('dp', 'tensor'), may hold values from -16 to 16
Outputs:
- inverses: float32 [16, 2, 8, 768, 768], P('section', 'tensor', 'dp')
All inputs are finite; a program needn't handle non-finite values. Where the computation divides by a largest or mean magnitude, that divisor is 1e-20 or more.
Results may differ from a plain program's by a relative error of at most 0.0003.
Values may be sent and summed in bfloat16 or wider, within the bound.
No kernel may reach another device: no remote copies, remote signals or barrier semaphores. Data moves between devices by JAX's collectives and lax.ppermute only.
A program may use at most 128 MiB of HBM per device.

v0:
```python
import jax
import jax.numpy as jnp
from jax import lax
from jax.sharding import PartitionSpec as P

D = 6144
BLK = 768
ITERS = 3


def from_behind(block, axis, distance):
    devices = range(lax.axis_size(axis))
    route = [(i - distance, i) for i in devices if i - distance in devices]
    return lax.ppermute(block, axis, route)


def invert(damped):
    row_bound = jnp.max(jnp.sum(jnp.abs(damped), axis=2), axis=1)[:, None, None]
    normed = damped / row_bound
    iterate = 2.0 * jnp.eye(BLK, dtype=jnp.float32) - normed
    for repeat in range(ITERS - 1):
        product = jnp.einsum("cij,cjk->cik", normed, iterate, precision=lax.Precision.HIGHEST)
        iterate = 2.0 * iterate - jnp.einsum(
            "cij,cjk->cik", iterate, product, precision=lax.Precision.HIGHEST
        )
    return iterate / row_bound


def per_device(embeddings, section_outputs, norm_gain, input_grads, loss_grads):
    section_place = lax.axis_index("section")
    arrived = from_behind(section_outputs, "section", 1)[0]
    returned = from_behind(input_grads, "section", -1)[0]
    hidden_rows = jnp.where(section_place == 0, embeddings, arrived)
    grad_rows = jnp.where(section_place == lax.axis_size("section") - 1, loss_grads, returned)
    row_values = hidden_rows.astype(jnp.float32)
    stat_sums = lax.psum(
        (
            jnp.sum(row_values, axis=1, keepdims=True),
            jnp.sum(row_values * row_values, axis=1, keepdims=True),
        ),
        "tensor",
    )
    row_mean = stat_sums[0] / D
    row_power = stat_sums[1] / D
    inputs = (
        (row_values - row_mean) * lax.rsqrt(row_power - row_mean * row_mean + 1e-05) * norm_gain[0]
    ).astype(jnp.bfloat16)
    stacked = jnp.stack([inputs, grad_rows])
    block_count = D // BLK // lax.axis_size("dp")
    total_tokens = hidden_rows.shape[0] * lax.axis_size("dp")
    gathered = lax.all_to_all(stacked, "tensor", split_axis=0, concat_axis=2, tiled=True)[0]
    segment = gathered
    segment = segment.reshape(segment.shape[0], block_count * lax.axis_size("dp"), BLK)
    factor = (
        lax.psum_scatter(
            jnp.einsum("tcb,tcd->cbd", segment, segment, preferred_element_type=jnp.float32),
            "dp",
            scatter_dimension=0,
            tiled=True,
        )
        / total_tokens
    )
    damped = factor + 0.05 * jnp.eye(BLK, dtype=jnp.float32)
    result = invert(damped)
    return result.reshape(1, 1, block_count, BLK, BLK)


def solution(mesh):
    placed = (
        P("dp", "tensor"),
        P("section", "dp", "tensor"),
        P("section", "tensor"),
        P("section", "dp", "tensor"),
        P("dp", "tensor"),
    )
    return jax.shard_map(
        per_device,
        mesh=mesh,
        in_specs=placed,
        out_specs=P("section", "tensor", "dp", None, None),
        check_vma=False,
    )
```

profile of v0, /device:TPU:1, one launch (start us, length us, event | category | flops | bytes accessed | tf_op | source)
XLA Modules:
  0.0 328.2 jit_solution(7038351599623615230)
XLA Ops:
  6.5 0.0 copy-start.1
  6.5 0.0 reduce-scatter.2.cloned.1.call-start
  6.5 2.7 copy.7
  9.2 4.9 %collective-permute-start = (bf16[1,256,3072]{1,2,0:T(8,128)(2,1)}, bf16[1,256,3072]{1,2,0:T(8,128)(2,1)}, u32[]{:S(2)}, u32[]{:S(2)}) collective-permute-start(bf16[1,256,3072]{1,2,0:T(8,128)(2,1)} %copy.7), channel_id=1, source_target_pairs={{0,16},{16,32},{32,48},{48,64},{64,80},{80,96},{96,112},{112,128},... | collective-permute-start | bytes 4718600 | tf_op jit(solution)/shard_map/ppermute | solution.py:14
  14.2 0.0 copy-done.1
  14.2 1.6 copy.9
  15.7 2.6 collective-permute-start.1
  18.4 1.7 copy.8
  20.1 1.7 copy.10
  21.8 0.0 copy-start.2
  21.8 10.0 %collective-permute-done = bf16[1,256,3072]{1,2,0:T(8,128)(2,1)} collective-permute-done((bf16[1,256,3072]{1,2,0:T(8,128)(2,1)}, bf16[1,256,3072]{1,2,0:T(8,128)(2,1)}, u32[]{:S(2)}, u32[]{:S(2)}) %collective-permute-start) | collective-permute-done | bytes 1572896 | tf_op jit(solution)/shard_map/ppermute | solution.py:14
  31.8 3.2 convert_reduce_fusion
  35.0 5.3 %all-reduce = (f32[256,1]{0,1:T(1,128)S(1)}, f32[256,1]{0,1:T(1,128)S(1)}) all-reduce(f32[256,1]{0,1:T(1,128)S(1)} %bitcast.57, f32[256,1]{0,1:T(1,128)S(1)} %bitcast.56), channel_id=1, replica_groups=mesh['section'=16,'dp'=8,'tensor'=2] {'tensor'}, use_global_device_ids=true, to_apply=%region_3.4 | all-reduce | flops 512 | bytes 4096 | tf_op jit(solution)/shard_map/psum | solution.py:36
  40.3 0.0 copy-done.2
  40.3 1.9 fusion.19
  42.3 0.0 collective-permute-done.1
  42.3 1.6 fusion.20
  43.9 0.3 pad_maximum_fusion
  44.2 31.8 %all_to_all.15 = bf16[2,256,3072]{1,2,0:T(8,128)(2,1)S(1)} all-to-all(bf16[2,256,3072]{1,2,0:T(8,128)(2,1)S(1)} %pad_maximum_fusion), channel_id=1, replica_groups=mesh['section'=16,'dp'=8,'tensor'=2] {'tensor'}, dimensions={0} | all-to-all | bytes 6291456 | tf_op jit(solution)/shard_map/all_to_all | solution.py:51
  76.0 7.9 %fusion.34 = f32[8,768,768]{2,1,0:T(8,128)} fusion(bf16[256,8,768]{0,2,1:T(8,128)(2,1)S(1)} %bitcast.54), kind=kOutput, calls=%fused_computation.41 | convolution fusion | flops 2415919104 | bytes 22020096 | tf_op jit(solution)/shard_map/tcb,tcd->cbd/dot_general | solution.py:56
  83.9 0.0 reduce-scatter.2.cloned.1.call-update
  83.9 203.3 %reduce-scatter.2.cloned.1.call-done = f32[1,768,768]{2,1,0:T(8,128)} async-done(((f32[8,768,768]{2,1,0:T(8,128)}), f32[1,768,768]{2,1,0:T(8,128)}) %reduce-scatter.2.cloned.1.call-update) | async-done | bytes 2359312 | tf_op jit(solution)/shard_map/reduce_scatter | solution.py:55
  287.3 2.0 abs_reduce_fusion
  289.3 0.7 reduce_max.9
  290.0 0.0 copy-start
  290.0 9.4 %fusion.11 = f32[768,768]{1,0:T(8,128)S(1)} fusion(f32[1,768,768]{2,1,0:T(8,128)} %reduce-scatter.2.cloned.1.call-done, f32[]{:T(128)} %reduce_max.9), kind=kOutput, calls=%fused_computation.17 | convolution fusion | flops 5442895872 | bytes 4718596 | tf_op jit(solution)/shard_map/cij,cjk->cik/dot_general | solution.py:22
  299.4 0.0 copy-done
  299.4 7.0 %bitcast_subtract_fusion.1 = f32[1,768,768]{2,1,0:T(8,128)S(1)} fusion(f32[768,768]{1,0:T(8,128)S(1)} %fusion.11, f32[]{:T(128)} %reduce_max.9, f32[1,768,768]{2,1,0:T(8,128)S(1)} %copy-done), kind=kOutput, calls=%fused_computation.15 | convolution fusion | flops 5445255168 | bytes 7077892 | tf_op jit(solution)/shard_map/cij,cjk->cik/dot_general | solution.py:23
  306.4 6.9 %fusion.8 = f32[768,768]{1,0:T(8,128)S(1)} fusion(f32[1,768,768]{2,1,0:T(8,128)S(1)} %bitcast_subtract_fusion.1, f32[1,768,768]{2,1,0:T(8,128)S(1)} %copy-done, f32[]{:T(128)} %reduce_max.9), kind=kOutput, calls=%fused_computation.13 | convolution fusion | flops 5438767104 | bytes 7077892 | tf_op jit(solution)/shard_map/cij,cjk->cik/dot_general | solution.py:22
  313.3 8.1 %fusion.5 = f32[1,1,1,768,768]{4,3,2,1,0:T(8,128)} fusion(f32[1,768,768]{2,1,0:T(8,128)S(1)} %bitcast_subtract_fusion.1, f32[768,768]{1,0:T(8,128)S(1)} %fusion.8, f32[]{:T(128)} %reduce_max.9), kind=kOutput, calls=%fused_computation.10 | convolution fusion | flops 5437587456 | bytes 7077892 | tf_op jit(solution)/shard_map/cij,cjk->cik/dot_general | solution.py:23
  (1 shorter events, 0.0 us)
Async XLA Ops:
  6.5 7.6 %copy-start.1 = (bf16[1,256,3072]{2,1,0:T(8,128)(2,1)S(1)}, bf16[1,256,3072]{2,1,0:T(8,128)(2,1)}, u32[]{:S(2)}) copy-start(bf16[1,256,3072]{2,1,0:T(8,128)(2,1)} %param.8) | copy-start | bytes 4718596
  6.5 280.7 %reduce-scatter.2.cloned.1.call-start = ((), (), s32[]{:S(2)}) async-start(), calls=%async_computation.2 | async-start | bytes 21233664 | tf_op jit(solution)/shard_map/reduce_scatter | solution.py:55
  9.2 22.6 %collective-permute-start = (bf16[1,256,3072]{1,2,0:T(8,128)(2,1)}, bf16[1,256,3072]{1,2,0:T(8,128)(2,1)}, u32[]{:S(2)}, u32[]{:S(2)}) collective-permute-start(bf16[1,256,3072]{1,2,0:T(8,128)(2,1)} %copy.7), channel_id=1, source_target_pairs={{0,16},{16,32},{32,48},{48,64},{64,80},{80,96},{96,112},{112,128},... | collective-permute-start | bytes 4718600 | tf_op jit(solution)/shard_map/ppermute | solution.py:14
  15.7 26.5 %collective-permute-start.1 = (bf16[1,256,3072]{1,2,0:T(8,128)(2,1)}, bf16[1,256,3072]{1,2,0:T(8,128)(2,1)}, u32[]{:S(2)}, u32[]{:S(2)}) collective-permute-start(bf16[1,256,3072]{1,2,0:T(8,128)(2,1)} %copy.9), channel_id=1, source_target_pairs={{16,0},{32,16},{48,32},{64,48},{80,64},{96,80},{112,96},{128,112},... | collective-permute-start | bytes 4718600 | tf_op jit(solution)/shard_map/ppermute | solution.py:14
  21.8 18.5 %copy-start.2 = (f32[1,3072]{1,0:T(1,128)S(1)}, f32[1,3072]{1,0:T(1,128)}, u32[]{:S(2)}) copy-start(f32[1,3072]{1,0:T(1,128)} %param.7) | copy-start | bytes 36868
  290.0 9.4 %copy-start = (f32[1,768,768]{2,1,0:T(8,128)S(1)}, f32[1,768,768]{2,1,0:T(8,128)}, u32[]{:S(2)}) copy-start(f32[1,768,768]{2,1,0:T(8,128)} %reduce-scatter.2.cloned.1.call-done) | copy-start | bytes 7077892
Sparse Core Ops, SparseCore 0:
  84.0 203.1 reduce-scatter.1
where the time goes:
time: 329 us; the launch traced here: 328 us
  waiting for transfers between devices  213 us (65%)
  matrix products  39.3 us (12%)
  blocking collectives  37.1 us (11%)
  between operations  13.5 us (4%)
  other arithmetic  9.75 us (3%)
  local copies, waits for them, and re-layouts  7.68 us (2%)
  starting transfers between devices  7.55 us (2%)
    reduce_scatter x1, waiting for transfers between devices, per_device(): lax.psum_scatter(jnp.einsum('tcb,tcd->cbd', segment, segment, preferred_e...  203 us
    all_to_all x1, blocking collectives, per_device(): lax.all_to_all(stacked, 'tensor', split_axis=0, concat_axis=2, tiled=True)  31.8 us
    dot_general x2, matrix products, invert(): jnp.einsum('cij,cjk->cik', normed, iterate, precision=lax.Precision.HIGHEST)  16.3 us
    dot_general x2, matrix products, invert(): jnp.einsum('cij,cjk->cik', iterate, product, precision=lax.Precision.HIGH...  15 us
    ppermute x2, waiting for transfers between devices, from_behind(): return lax.ppermute(block, axis, route)  10 us
    dot_general x1, matrix products, per_device(): jnp.einsum('tcb,tcd->cbd', segment, segment, preferred_element_type=jnp.f...  7.9 us
    unnamed x10, local copies, waits for them, and re-layouts  7.68 us
    ppermute x2, starting transfers between devices, from_behind(): return lax.ppermute(block, axis, route)  7.55 us
  transfers between devices with their start and end apart: 3, of which 2 were waited for; matrix products, arithmetic and copies ran while one was open for 3% of the time, Pallas kernels for 0%

commit v1 on v0

v1 whole, which is shorter than its diff:
```python
import functools

import jax
import jax.numpy as jnp
from jax import lax
from jax.experimental import pallas as pl
from jax.experimental.pallas import tpu as pltpu
from jax.sharding import PartitionSpec as P

D = 6144
BLK = 768
TOKENS = 2048
SECTIONS, REPLICAS, HALVES = 16, 8, 2
ROWS = TOKENS // REPLICAS
COLS = D // HALVES
AXES = ("section", "dp", "tensor")
ROUNDS = [(rx, rk) for rk in range(2) for rx in range(4)]


def device_index(s, d, h):
    return (s * REPLICAS + d) * HALVES + h


def route(rx, rk):
    pairs = []
    for s in range(SECTIONS):
        for d in range(REPLICAS):
            for h in range(HALVES):
                kind = (d // 4) ^ rk
                j = (d % 4 + rx) % 4
                to = (s + 1) % SECTIONS if kind == 0 else (s - 1) % SECTIONS
                pairs.append((device_index(s, d, h), device_index(to, 4 * h + j, kind)))
    return pairs


def chunk_kernel(emb, outs, grads, loss, *rest):
    chunks, sems = rest[:8], rest[8]
    s = lax.axis_index("section")
    d = lax.axis_index("dp")
    x, ylo = lax.rem(d, 4), lax.div(d, 4)

    def copies(r, src):
        rx, rk = ROUNDS[r]
        j = lax.rem(x + rx, 4)
        cols = pl.ds(pl.multiple_of(j * BLK, BLK), BLK)
        return pltpu.make_async_copy(src.at[:, cols], chunks[r], sems.at[r])

    for r, (rx, rk) in enumerate(ROUNDS):
        kind = lax.rem(ylo + rk, 2)
        edge = jnp.where(kind == 0, s == SECTIONS - 1, s == 0)
        for k, e, src in ((0, True, emb), (0, False, outs), (1, True, loss), (1, False, grads)):
            @pl.when((kind == k) & (edge == e))
            def _():
                copies(r, src).start()
    for r in range(8):
        copies(r, outs).wait()


def make_chunks(emb, outs, grads, loss):
    any_spec = pl.BlockSpec(memory_space=pl.ANY)
    return pl.pallas_call(
        chunk_kernel,
        out_shape=[jax.ShapeDtypeStruct((ROWS, BLK), jnp.bfloat16)] * 8,
        in_specs=[any_spec] * 4,
        out_specs=[any_spec] * 8,
        scratch_shapes=[pltpu.SemaphoreType.DMA((8,))],
        name="chunks",
    )(emb, outs, grads, loss)


def gram_kernel(acc, chunk, mean, scale, gain, out):
    rows = chunk[...].astype(jnp.float32)
    rows = ((rows - mean[...]) * scale[...] * gain[...]).astype(jnp.bfloat16)
    part = lax.dot_general(
        rows, rows, (((0,), (0,)), ((), ())), preferred_element_type=jnp.float32
    )
    if acc is None:
        out[...] = part
    else:
        out[...] = acc[...] + part


def gram(acc, chunk, mean, scale, gain):
    vmem = pl.BlockSpec(memory_space=pltpu.VMEM)
    args = [chunk, mean, scale, gain]
    body = functools.partial(gram_kernel, None)
    aliases = {}
    if acc is not None:
        args = [acc] + args
        body = gram_kernel
        aliases = {0: 0}
    return pl.pallas_call(
        body,
        out_shape=jax.ShapeDtypeStruct((BLK, BLK), jnp.float32),
        in_specs=[vmem] * len(args),
        out_specs=vmem,
        input_output_aliases=aliases,
        compiler_params=pltpu.CompilerParams(vmem_limit_bytes=32 * 2**20),
        name="gram",
    )(*args)


def split(a):
    hi = a.astype(jnp.bfloat16)
    return hi, (a - hi.astype(jnp.float32)).astype(jnp.bfloat16)


def times(a, b):
    def dot(p, q):
        return jnp.dot(p, q, preferred_element_type=jnp.float32)

    return dot(a[0], b[0]) + (dot(a[0], b[1]) + dot(a[1], b[0]))


def invert_kernel(total, out):
    row = lax.broadcasted_iota(jnp.int32, (BLK, BLK), 0)
    col = lax.broadcasted_iota(jnp.int32, (BLK, BLK), 1)
    eye = jnp.where(row == col, 1.0, 0.0).astype(jnp.float32)
    damped = total[...] * (1.0 / TOKENS) + 0.05 * eye
    bound = jnp.max(jnp.sum(jnp.abs(damped), axis=1, keepdims=True))
    first = eye - damped / bound
    first_parts = split(first)
    second = times(first_parts, first_parts)
    second_parts = split(second)
    low = eye + first + second + times(first_parts, second_parts)
    fourth = times(second_parts, second_parts)
    out[...] = (low + times(split(low), split(fourth))) / bound


def invert(total):
    vmem = pl.BlockSpec(memory_space=pltpu.VMEM)
    return pl.pallas_call(
        invert_kernel,
        out_shape=jax.ShapeDtypeStruct((BLK, BLK), jnp.float32),
        in_specs=[vmem],
        out_specs=vmem,
        compiler_params=pltpu.CompilerParams(vmem_limit_bytes=48 * 2**20),
        name="invert",
    )(total)


def per_device(embeddings, section_outputs, norm_gain, input_grads, loss_grads):
    s = lax.axis_index("section")
    d = lax.axis_index("dp")
    h = lax.axis_index("tensor")
    sent = section_outputs[0]
    chunks = make_chunks(embeddings, sent, input_grads[0], loss_grads)
    arrived = [lax.ppermute(c, AXES, route(*r)) for c, r in zip(chunks, ROUNDS)]

    other_gain = lax.ppermute(norm_gain, "tensor", [(0, 1), (1, 0)])
    gain_half = jnp.where(d // 4 == 0, norm_gain, other_gain)
    gain = lax.dynamic_slice(gain_half, (0, (d % 4) * BLK), (1, BLK))
    gain = jnp.where(h == 0, gain, 1.0)

    values = jnp.where(s == SECTIONS - 1, embeddings, sent).astype(jnp.float32)
    sums = jnp.stack([jnp.sum(values, axis=1), jnp.sum(values * values, axis=1)])
    gathered = lax.all_gather(sums, ("dp", "tensor"))
    stats = jnp.sum(gathered.reshape(REPLICAS, HALVES, 2, ROWS), axis=1)
    stats = lax.ppermute(stats, "section", [(i, (i + 1) % SECTIONS) for i in range(SECTIONS)])
    mean = stats[:, 0] / D
    power = stats[:, 1] / D
    scale = lax.rsqrt(power - mean * mean + 1e-05)
    mean = jnp.where(h == 0, mean, 0.0)[:, :, None]
    scale = jnp.where(h == 0, scale, 1.0)[:, :, None]

    total = None
    for chunk, (rx, rk) in zip(arrived, ROUNDS):
        source = (h ^ rk) * 4 + (d % 4 + 4 - rx) % 4
        total = gram(
            total,
            chunk,
            lax.dynamic_index_in_dim(mean, source, 0, False),
            lax.dynamic_index_in_dim(scale, source, 0, False),
            gain,
        )
    return invert(total).reshape(1, 1, 1, BLK, BLK)


def solution(mesh):
    placed = (
        P("dp", "tensor"),
        P("section", "dp", "tensor"),
        P("section", "tensor"),
        P("section", "dp", "tensor"),
        P("dp", "tensor"),
    )
    return jax.shard_map(
        per_device,
        mesh=mesh,
        in_specs=placed,
        out_specs=P("section", "tensor", "dp", None, None),
        check_vma=False,
    )
```

time: 329 us -> 233 us (0.71); the launches traced: 328 us -> 228 us
  waiting for transfers between devices: 213 us -> 22.6 us
  Pallas kernels: 0 us -> 125 us
  matrix products: 39.3 us -> 0 us
  starting transfers between devices: 7.55 us -> 36.1 us
  between operations: 13.5 us -> 0.25 us
  other arithmetic: 9.75 us -> 2.21 us
  local copies, waits for them, and re-layouts: 7.68 us -> 2.25 us
    reduce_scatter x1 -> x0, waiting for transfers between devices: 203 us -> none  [per_device(): lax.psum_scatter(jnp.einsum('tcb,tcd->cbd', segment, segment, preferred_e...]
    pallas_call x0 -> x10, Pallas kernels: none -> 125 us  [the longest x1 96.5 us: make_chunks(): pl.pallas_call(chunk_kernel, out_shape=[jax.ShapeDtypeStruct((ROWS, BLK),...]
    all_gather x0 -> x1, blocking collectives: none -> 39.6 us  [per_device(): gathered = lax.all_gather(sums, ('dp', 'tensor'))]
    dot_general x5 -> x0, matrix products: 39.3 us -> none  [the longest x2 16.3 us: invert(): jnp.einsum('cij,cjk->cik', normed, iterate, precision=lax.Precision.HIGHEST)]
    all_to_all x1 -> x0, blocking collectives: 31.8 us -> none  [per_device(): lax.all_to_all(stacked, 'tensor', split_axis=0, concat_axis=2, tiled=True)]
    ppermute x2 -> x10, starting transfers between devices: 7.55 us -> 36.1 us  [the longest x8 22.5 us: per_device(): arrived = [lax.ppermute(c, AXES, route(*r)) for c, r in zip(chunks, ROUNDS)]]
    ppermute x2 -> x10, waiting for transfers between devices: 10 us -> 22.6 us  [the longest x8 21.5 us: per_device(): arrived = [lax.ppermute(c, AXES, route(*r)) for c, r in zip(chunks, ROUNDS)]]
    unnamed x10 -> x4, local copies, waits for them, and re-layouts: 7.68 us -> 0.01 us
  transfers between devices with their start and end apart: 3 -> 10, of which waited for: 2 -> 3; matrix products, arithmetic and copies ran while one was open for 3% -> 2% of each run, Pallas kernels for 0% -> 4%
where the time goes in v1:
time: 233 us; the launch traced here: 228 us
  Pallas kernels  125 us (54%)
  blocking collectives  39.6 us (17%)
  starting transfers between devices  36.1 us (15%)
  waiting for transfers between devices  22.6 us (10%)
    pallas_call x1, Pallas kernels, make_chunks(): pl.pallas_call(chunk_kernel, out_shape=[jax.ShapeDtypeStruct((ROWS, BLK),...  96.5 us
    all_gather x1, blocking collectives, per_device(): gathered = lax.all_gather(sums, ('dp', 'tensor'))  39.6 us
    ppermute x8, starting transfers between devices, per_device(): arrived = [lax.ppermute(c, AXES, route(*r)) for c, r in zip(chunks, ROUNDS)]  22.5 us
    ppermute x8, waiting for transfers between devices, per_device(): arrived = [lax.ppermute(c, AXES, route(*r)) for c, r in zip(chunks, ROUNDS)]  21.5 us
    pallas_call x1, Pallas kernels, invert(): pl.pallas_call(invert_kernel, out_shape=jax.ShapeDtypeStruct((BLK, BLK),...  17.5 us
    pallas_call x8, Pallas kernels, gram(): pl.pallas_call(body, out_shape=jax.ShapeDtypeStruct((BLK, BLK), jnp.float...  11.1 us
    ppermute x1, starting transfers between devices, per_device(): lax.ppermute(stats, 'section', [(i, (i + 1) % SECTIONS) for i in range(SE...  10.1 us
  transfers between devices with their start and end apart: 10, of which 3 were waited for; matrix products, arithmetic and copies ran while one was open for 2% of the time, Pallas kernels for 4%

profile of v1, /device:TPU:1, one launch (start us, length us, event | category | flops | bytes accessed | tf_op | source)
XLA Modules:
  0.0 228.1 jit_solution(5300524344035702073)
XLA Ops:
  0.0 96.5 %chunks.1 = (bf16[256,768]{1,0:T(8,128)(2,1)}, bf16[256,768]{1,0:T(8,128)(2,1)}, bf16[256,768]{1,0:T(8,128)(2,1)}, bf16[256,768]{1,0:T(8,128)(2,1)}, bf16[256,76...) custom-call(bf16[256,3072]{1,0:T(8,128)(2,1)} %emb.1, ...), custom_call_target="tpu_custom_call" | custom-call | tf_op jit(solution)/shard_map/chunks/pallas_call | solution.py:61
  96.5 3.1 %collective-permute-start = (bf16[256,768]{1,0:T(8,128)(2,1)}, bf16[256,768]{1,0:T(8,128)(2,1)S(1)}, u32[]{:S(2)}, u32[]{:S(2)}) collective-permute-start(bf16[256,768]{1,0:T(8,128)(2,1)} %get-tuple-element.13), channel_id=1, source_target_pairs={{0,16},{1,24},{2,18},{3,26},{4,20},{5,28},{6,22},{7,30},{8,241},{9... | collective-permute-start | bytes 1179656 | tf_op jit(solution)/shard_map/ppermute | solution.py:148
  99.6 1.0 collective-permute-start.3
  100.6 4.3 %collective-permute-start.4 = (bf16[256,768]{1,0:T(8,128)(2,1)}, bf16[256,768]{1,0:T(8,128)(2,1)S(1)}, u32[]{:S(2)}, u32[]{:S(2)}) collective-permute-start(bf16[256,768]{1,0:T(8,128)(2,1)} %get-tuple-element.15), channel_id=1, source_target_pairs={{0,20},{1,28},{2,22},{3,30},{4,16},{5,24},{6,18},{7,26},{8,245},{9... | collective-permute-start | bytes 1179656 | tf_op jit(solution)/shard_map/ppermute | solution.py:148
  104.9 2.1 convert_reduce_fusion
  107.0 39.6 %all-gather.1 = f32[16,2,256]{2,1,0:T(2,128)S(1)} all-gather(f32[1,2,256]{2,1,0:T(2,128)S(1)} %maximum_bitcast_fusion), channel_id=2, replica_groups=mesh['section'=16,'dp'=8,'tensor'=2] {'dp','tensor'}, dimensions={0}, use_global_device_ids=true | all-gather | bytes 34816 | tf_op jit(solution)/shard_map/all_gather | solution.py:157
  146.7 10.1 %collective-permute-start.1 = (f32[8,2,256]{2,1,0:T(2,128)S(1)}, f32[8,2,256]{2,1,0:T(2,128)S(1)}, u32[]{:S(2)}, u32[]{:S(2)}) collective-permute-start(f32[8,2,256]{2,1,0:T(2,128)S(1)} %bitcast_reduce_fusion), channel_id=1, source_target_pairs={{0,16},{16,32},{32,48},{48,64},{64,80},{80,96},{96,112},{112,128},... | collective-permute-start | bytes 49160 | tf_op jit(solution)/shard_map/ppermute | solution.py:159
  156.7 3.5 %collective-permute-start.2 = (f32[1,3072]{1,0:T(1,128)S(1)}, f32[1,3072]{1,0:T(1,128)S(1)}, u32[]{:S(2)}, u32[]{:S(2)}) collective-permute-start(f32[1,3072]{1,0:T(1,128)S(1)} %copy-done.1), channel_id=1, source_target_pairs={{0,1},{1,0},{2,3},{3,2},{4,5},{5,4},{6,7},{7,6},{8,9},{9,8},{10,11... | collective-permute-start | bytes 36872 | tf_op jit(solution)/shard_map/ppermute | solution.py:150
  160.2 1.1 collective-permute-done.2
  161.3 3.4 %collective-permute-start.5 = (bf16[256,768]{1,0:T(8,128)(2,1)}, bf16[256,768]{1,0:T(8,128)(2,1)}, u32[]{:S(2)}, u32[]{:S(2)}) collective-permute-start(bf16[256,768]{1,0:T(8,128)(2,1)} %get-tuple-element.16), channel_id=1, source_target_pairs={{0,22},{1,30},{2,16},{3,24},{4,18},{5,26},{6,20},{7,28},{8,247},{9... | collective-permute-start | bytes 1179656 | tf_op jit(solution)/shard_map/ppermute | solution.py:148
  164.7 7.8 %collective-permute-start.7 = (bf16[256,768]{1,0:T(8,128)(2,1)}, bf16[256,768]{1,0:T(8,128)(2,1)}, u32[]{:S(2)}, u32[]{:S(2)}) collective-permute-start(bf16[256,768]{1,0:T(8,128)(2,1)} %get-tuple-element.18), channel_id=1, source_target_pairs={{0,243},{1,251},{2,245},{3,253},{4,247},{5,255},{6,241},{7,249},{8... | collective-permute-start | bytes 1179656 | tf_op jit(solution)/shard_map/ppermute | solution.py:148
  172.5 1.5 collective-permute-start.8
  174.1 1.4 collective-permute-start.9
  175.7 0.1 copy.30.scale
  175.9 0.1 copy.31.mean
  176.0 0.1 copy.32.scale
  176.2 0.1 copy.33.mean
  176.3 0.1 copy.34.scale
  176.5 0.1 copy.35.mean
  176.6 0.1 copy.36.scale
  176.7 0.1 copy.37.mean
  177.9 0.7 gram.8.acc
  178.6 0.8 gram.9.acc
  179.4 0.8 gram.10.acc
  180.2 1.8 gram.11.acc
  181.9 20.5 %collective-permute-done.6.chunk = bf16[256,768]{1,0:T(8,128)(2,1)} collective-permute-done((bf16[256,768]{1,0:T(8,128)(2,1)}, bf16[256,768]{1,0:T(8,128)(2,1)}, u32[]{:S(2)}, u32[]{:S(2)}) %collective-permute-start.6) | collective-permute-done | bytes 393248 | tf_op jit(solution)/shard_map/ppermute | solution.py:148
  202.4 1.8 gram.12.acc
  204.2 1.8 gram.13.acc
  206.0 1.0 collective-permute-done.8.chunk
  207.0 1.8 gram.14.acc
  208.8 1.8 gram.15.total
  210.6 17.5 %invert.1 = f32[768,768]{1,0:T(8,128)} custom-call(f32[768,768]{1,0:T(8,128)S(1)} %gram.15.total), custom_call_target="tpu_custom_call" | custom-call | tf_op jit(solution)/shard_map/invert/pallas_call | solution.py:132
  (25 shorter events, 1.2 us)
Async XLA Ops:
  0.0 104.9 %copy-start = (bf16[256,3072]{1,0:T(8,128)(2,1)S(1)}, bf16[256,3072]{1,0:T(8,128)(2,1)}, u32[]{:S(2)}) copy-start(bf16[256,3072]{1,0:T(8,128)(2,1)} %emb.1) | copy-start | bytes 4718596
  96.5 60.3 %copy-start.1 = (f32[1,3072]{1,0:T(1,128)S(1)}, f32[1,3072]{1,0:T(1,128)}, u32[]{:S(2)}) copy-start(f32[1,3072]{1,0:T(1,128)} %param.7) | copy-start | bytes 36868
  96.5 68.2 %collective-permute-start = (bf16[256,768]{1,0:T(8,128)(2,1)}, bf16[256,768]{1,0:T(8,128)(2,1)S(1)}, u32[]{:S(2)}, u32[]{:S(2)}) collective-permute-start(bf16[256,768]{1,0:T(8,128)(2,1)} %get-tuple-element.13), channel_id=1, source_target_pairs={{0,16},{1,24},{2,18},{3,26},{4,20},{5,28},{6,22},{7,30},{8,241},{9... | collective-permute-start | bytes 1179656 | tf_op jit(solution)/shard_map/ppermute | solution.py:148
  99.6 72.9 %collective-permute-start.3 = (bf16[256,768]{1,0:T(8,128)(2,1)}, bf16[256,768]{1,0:T(8,128)(2,1)S(1)}, u32[]{:S(2)}, u32[]{:S(2)}) collective-permute-start(bf16[256,768]{1,0:T(8,128)(2,1)} %get-tuple-element.14), channel_id=1, source_target_pairs={{0,18},{1,26},{2,20},{3,28},{4,22},{5,30},{6,16},{7,24},{8,243},{9... | collective-permute-start | bytes 1179656 | tf_op jit(solution)/shard_map/ppermute | solution.py:148
  100.6 73.5 %collective-permute-start.4 = (bf16[256,768]{1,0:T(8,128)(2,1)}, bf16[256,768]{1,0:T(8,128)(2,1)S(1)}, u32[]{:S(2)}, u32[]{:S(2)}) collective-permute-start(bf16[256,768]{1,0:T(8,128)(2,1)} %get-tuple-element.15), channel_id=1, source_target_pairs={{0,20},{1,28},{2,22},{3,30},{4,16},{5,24},{6,18},{7,26},{8,245},{9... | collective-permute-start | bytes 1179656 | tf_op jit(solution)/shard_map/ppermute | solution.py:148
  146.7 18.0 %collective-permute-start.1 = (f32[8,2,256]{2,1,0:T(2,128)S(1)}, f32[8,2,256]{2,1,0:T(2,128)S(1)}, u32[]{:S(2)}, u32[]{:S(2)}) collective-permute-start(f32[8,2,256]{2,1,0:T(2,128)S(1)} %bitcast_reduce_fusion), channel_id=1, source_target_pairs={{0,16},{16,32},{32,48},{48,64},{64,80},{80,96},{96,112},{112,128},... | collective-permute-start | bytes 49160 | tf_op jit(solution)/shard_map/ppermute | solution.py:159
  156.7 4.6 %collective-permute-start.2 = (f32[1,3072]{1,0:T(1,128)S(1)}, f32[1,3072]{1,0:T(1,128)S(1)}, u32[]{:S(2)}, u32[]{:S(2)}) collective-permute-start(f32[1,3072]{1,0:T(1,128)S(1)} %copy-done.1), channel_id=1, source_target_pairs={{0,1},{1,0},{2,3},{3,2},{4,5},{5,4},{6,7},{7,6},{8,9},{9,8},{10,11... | collective-permute-start | bytes 36872 | tf_op jit(solution)/shard_map/ppermute | solution.py:150
  161.3 18.8 %collective-permute-start.5 = (bf16[256,768]{1,0:T(8,128)(2,1)}, bf16[256,768]{1,0:T(8,128)(2,1)}, u32[]{:S(2)}, u32[]{:S(2)}) collective-permute-start(bf16[256,768]{1,0:T(8,128)(2,1)} %get-tuple-element.16), channel_id=1, source_target_pairs={{0,22},{1,30},{2,16},{3,24},{4,18},{5,26},{6,20},{7,28},{8,247},{9... | collective-permute-start | bytes 1179656 | tf_op jit(solution)/shard_map/ppermute | solution.py:148
  164.7 37.7 %collective-permute-start.6 = (bf16[256,768]{1,0:T(8,128)(2,1)}, bf16[256,768]{1,0:T(8,128)(2,1)}, u32[]{:S(2)}, u32[]{:S(2)}) collective-permute-start(bf16[256,768]{1,0:T(8,128)(2,1)} %get-tuple-element.17), channel_id=1, source_target_pairs={{0,241},{1,249},{2,243},{3,251},{4,245},{5,253},{6,247},{7,255},{8... | collective-permute-start | bytes 1179656 | tf_op jit(solution)/shard_map/ppermute | solution.py:148
  164.7 39.5 %collective-permute-start.7 = (bf16[256,768]{1,0:T(8,128)(2,1)}, bf16[256,768]{1,0:T(8,128)(2,1)}, u32[]{:S(2)}, u32[]{:S(2)}) collective-permute-start(bf16[256,768]{1,0:T(8,128)(2,1)} %get-tuple-element.18), channel_id=1, source_target_pairs={{0,243},{1,251},{2,245},{3,253},{4,247},{5,255},{6,241},{7,249},{8... | collective-permute-start | bytes 1179656 | tf_op jit(solution)/shard_map/ppermute | solution.py:148
  172.5 34.5 %collective-permute-start.8 = (bf16[256,768]{1,0:T(8,128)(2,1)}, bf16[256,768]{1,0:T(8,128)(2,1)}, u32[]{:S(2)}, u32[]{:S(2)}) collective-permute-start(bf16[256,768]{1,0:T(8,128)(2,1)} %get-tuple-element.19), channel_id=1, source_target_pairs={{0,245},{1,253},{2,247},{3,255},{4,241},{5,249},{6,243},{7,251},{8... | collective-permute-start | bytes 1179656 | tf_op jit(solution)/shard_map/ppermute | solution.py:148
  174.1 34.7 %collective-permute-start.9 = (bf16[256,768]{1,0:T(8,128)(2,1)}, bf16[256,768]{1,0:T(8,128)(2,1)}, u32[]{:S(2)}, u32[]{:S(2)}) collective-permute-start(bf16[256,768]{1,0:T(8,128)(2,1)} %get-tuple-element.20), channel_id=1, source_target_pairs={{0,247},{1,255},{2,241},{3,249},{4,243},{5,251},{6,245},{7,253},{8... | collective-permute-start | bytes 1179656 | tf_op jit(solution)/shard_map/ppermute | solution.py:148

commit v2 on v1

v2 whole, which is shorter than its diff:
```python
import functools

import jax
import jax.numpy as jnp
from jax import lax
from jax.experimental import pallas as pl
from jax.experimental.pallas import tpu as pltpu
from jax.sharding import PartitionSpec as P

D = 6144
BLK = 768
TOKENS = 2048
SECTIONS, REPLICAS, HALVES = 16, 8, 2
ROWS = TOKENS // REPLICAS
COLS = D // HALVES
AXES = ("section", "dp", "tensor")


def pairs(move):
    out = []
    for s in range(SECTIONS):
        for d in range(REPLICAS):
            for h in range(HALVES):
                to_s, x, y = move(s, d % 4, 2 * h + d // 4)
                to = ((to_s % SECTIONS) * REPLICAS + (y % 2) * 4 + x % 4) * HALVES + y // 2
                out.append(((s * REPLICAS + d) * HALVES + h, to))
    return out


def across(shift, own):
    def move(s, x, y):
        kind = y // 2 if own else 1 - y // 2
        return (s + 1 if kind == 0 else s - 1), x + shift, y

    return pairs(move)


SIGMA = pairs(lambda s, x, y: (s, x, y ^ 3))
TAU = pairs(lambda s, x, y: (s, x, y ^ 1))


def send(block, route):
    return lax.ppermute(block, AXES, route)


CUTS = [(False, 2), (False, 1), (False, 3), (True, 1), (True, 3), (False, 0), (True, 2), (True, 0)]


def cut_kernel(emb, outs, grads, loss, *rest):
    chunks, sems = rest[:-1], rest[-1]
    s = lax.axis_index("section")
    x = lax.rem(lax.axis_index("dp"), 4)
    h = lax.axis_index("tensor")

    def copy(r, src):
        j = lax.rem(x + CUTS[r][1], 4)
        cols = pl.ds(pl.multiple_of(j * BLK, BLK), BLK)
        return pltpu.make_async_copy(src.at[:, cols], chunks[r], sems.at[r])

    for r, (own, _) in enumerate(CUTS):
        kind = h if own else 1 - h
        edge = jnp.where(kind == 0, s == SECTIONS - 1, s == 0)
        for k, e, src in ((0, True, emb), (0, False, outs), (1, True, loss), (1, False, grads)):
            @pl.when((kind == k) & (edge == e))
            def _():
                copy(r, src).start()
    for r in range(len(CUTS)):
        copy(r, outs).wait()


def cut(emb, outs, grads, loss):
    any_spec = pl.BlockSpec(memory_space=pl.ANY)
    vmem = pl.BlockSpec(memory_space=pltpu.VMEM)
    return pl.pallas_call(
        cut_kernel,
        out_shape=[jax.ShapeDtypeStruct((ROWS, BLK), jnp.bfloat16)] * len(CUTS),
        in_specs=[any_spec] * 4,
        out_specs=[vmem] * len(CUTS),
        scratch_shapes=[pltpu.SemaphoreType.DMA((len(CUTS),))],
        name="cut",
    )(emb, outs, grads, loss)


def normed(chunk, mean, scale, gain):
    return ((chunk.astype(jnp.float32) - mean) * scale * gain).astype(jnp.bfloat16)


def pair_gram(first, second, sums, gain_row):
    is_input = lax.axis_index("tensor") == 0
    mean = sums[:, 0] / D
    power = sums[:, 1] / D
    scale = lax.rsqrt(power - mean * mean + 1e-05)
    mean = jnp.where(is_input, mean, 0.0)
    scale = jnp.where(is_input, scale, 1.0)
    gain = jnp.where(is_input, gain_row, 1.0)
    cols = jnp.concatenate([mean, scale, mean, scale], axis=0).T
    rows = jnp.concatenate(
        [
            normed(first, cols[:, 0:1], cols[:, 2:3], gain),
            normed(second, cols[:, 1:2], cols[:, 3:4], gain),
        ],
        axis=0,
    )
    return lax.dot_general(
        rows, rows, (((0,), (0,)), ((), ())), preferred_element_type=jnp.float32
    )


def is_keeper():
    return lax.axis_index("tensor") == lax.div(lax.axis_index("dp"), 4)


def gram_kernel(gain, sums2, k2, t2, sums0, k0, t0, out):
    out[...] = pair_gram(k2[...], t2[...], sums2[...], gain[...])
    out[...] += pair_gram(k0[...], t0[...], sums0[...], gain[...])


def gram_more_kernel(acc, gain, sums, b, a, t, out):
    kept = jnp.where(is_keeper(), b[...], a[...])
    out[...] = acc[...] + pair_gram(kept, t[...], sums[...], gain[...])


def split(a):
    hi = a.astype(jnp.bfloat16)
    return hi, (a - hi.astype(jnp.float32)).astype(jnp.bfloat16)


def times(a, b):
    def dot(p, q):
        return jnp.dot(p, q, preferred_element_type=jnp.float32)

    return dot(a[0], b[0]) + (dot(a[0], b[1]) + dot(a[1], b[0]))


def invert(total):
    row = lax.broadcasted_iota(jnp.int32, (BLK, BLK), 0)
    col = lax.broadcasted_iota(jnp.int32, (BLK, BLK), 1)
    eye = jnp.where(row == col, 1.0, 0.0).astype(jnp.float32)
    damped = total * (1.0 / TOKENS) + 0.05 * eye
    bound = jnp.max(jnp.sum(jnp.abs(damped), axis=1, keepdims=True))
    first = eye - damped / bound
    first_parts = split(first)
    second = times(first_parts, first_parts)
    second_parts = split(second)
    low = eye + first + second + times(first_parts, second_parts)
    fourth = times(second_parts, second_parts)
    return (low + times(split(low), split(fourth))) / bound


def last_kernel(acc, gain, sums, b, a, t, out):
    kept = jnp.where(is_keeper(), b[...], a[...])
    out[...] = invert(acc[...] + pair_gram(kept, t[...], sums[...], gain[...]))


def in_vmem(kernel, name, *args):
    vmem = pl.BlockSpec(memory_space=pltpu.VMEM)
    return pl.pallas_call(
        kernel,
        out_shape=jax.ShapeDtypeStruct((BLK, BLK), jnp.float32),
        in_specs=[vmem] * len(args),
        out_specs=vmem,
        compiler_params=pltpu.CompilerParams(vmem_limit_bytes=48 * 2**20),
        name=name,
    )(*args)


def per_device(embeddings, section_outputs, norm_gain, input_grads, loss_grads):
    s = lax.axis_index("section")
    d = lax.axis_index("dp")
    h = lax.axis_index("tensor")
    keeper = h == d // 4
    sent = section_outputs[0]

    a2, a1, a3, b1, b3, a0, b2, b0 = cut(embeddings, sent, input_grads[0], loss_grads)

    ra2 = send(a2, SIGMA)
    xa1 = send(a1, across(1, False))
    xa3 = send(a3, across(3, False))
    xb1 = send(b1, across(1, True))
    xb3 = send(b3, across(3, True))

    values = jnp.where(s == SECTIONS - 1, embeddings, sent).astype(jnp.float32)
    sums = jnp.stack([jnp.sum(values, axis=1), jnp.sum(values * values, axis=1)])
    other = send(jnp.concatenate([sums.reshape(1, -1), norm_gain], axis=1), SIGMA)
    crossed = other[0, : 2 * ROWS].reshape(2, ROWS)
    gain_half = jnp.where(d // 4 == 0, norm_gain, other[:, 2 * ROWS :])
    gain = lax.dynamic_slice(gain_half, (0, (d % 4) * BLK), (1, BLK))
    beside = send(jnp.stack([crossed, sums]), TAU)
    full = jnp.stack([sums, crossed]) + beside
    full = jnp.where(keeper, full, full[::-1])
    stats = {i: send(full, across(i, True)) for i in range(4)}

    t2 = jnp.where(keeper, ra2, b2)
    k2 = jnp.where(keeper, b2, ra2)
    t2 = send(t2, TAU)
    ra0 = send(a0, SIGMA)
    t0 = jnp.where(keeper, ra0, b0)
    k0 = jnp.where(keeper, b0, ra0)
    t0 = send(t0, TAU)
    ra1 = send(xa1, SIGMA)
    xk2 = send(k2, across(2, True))
    xt2 = send(t2, across(2, True))
    ra3 = send(xa3, SIGMA)
    t1 = send(jnp.where(keeper, ra1, xb1), TAU)
    xk0 = send(k0, across(0, True))
    xt0 = send(t0, across(0, True))
    t3 = send(jnp.where(keeper, ra3, xb3), TAU)

    total = in_vmem(gram_kernel, "gram20", gain, stats[2], xk2, xt2, stats[0], xk0, xt0)
    total = in_vmem(gram_more_kernel, "gram1", total, gain, stats[1], xb1, ra1, t1)
    result = in_vmem(last_kernel, "gram3", total, gain, stats[3], xb3, ra3, t3)
    return result.reshape(1, 1, 1, BLK, BLK)


def solution(mesh):
    placed = (
        P("dp", "tensor"),
        P("section", "dp", "tensor"),
        P("section", "tensor"),
        P("section", "dp", "tensor"),
        P("dp", "tensor"),
    )
    return jax.shard_map(
        per_device,
        mesh=mesh,
        in_specs=placed,
        out_specs=P("section", "tensor", "dp", None, None),
        check_vma=False,
    )
```

time: 233 us -> 98.7 us (0.42)
  the two profiles are of different devices: /device:TPU:1 before, /device:TPU:3 now
where the time goes in v2:
time: 98.7 us; the launch traced here: 98.4 us
  starting transfers between devices  49.7 us (50%)
  Pallas kernels  27.3 us (28%)
  waiting for transfers between devices  14.2 us (14%)
  other arithmetic  6.38 us (6%)
    ppermute x22, starting transfers between devices, send(): return lax.ppermute(block, AXES, route)  49.7 us
    pallas_call x3, Pallas kernels, in_vmem(): pl.pallas_call(kernel, out_shape=jax.ShapeDtypeStruct((BLK, BLK), jnp.flo...  23.7 us
    ppermute x22, waiting for transfers between devices, send(): return lax.ppermute(block, AXES, route)  14.2 us
    pallas_call x1, Pallas kernels, cut(): pl.pallas_call(cut_kernel, out_shape=[jax.ShapeDtypeStruct((ROWS, BLK), j...  3.59 us
    reduce_sum x1, other arithmetic, per_device(): jnp.sum(values, axis=1)  2.16 us
  transfers between devices with their start and end apart: 22, of which 8 were waited for; matrix products, arithmetic and copies ran while one was open for 5% of the time, Pallas kernels for 8%

profile of v2, /device:TPU:3, one launch (start us, length us, event | category | flops | bytes accessed | tf_op | source)
XLA Modules:
  0.0 98.4 jit_solution(15367688979875840970)
XLA Ops:
  0.0 2.2 %convert_reduce_fusion = (f32[256]{0:T(256)S(1)}, f32[256]{0:T(256)S(1)}) fusion(bf16[256,3072]{1,0:T(8,128)(2,1)} %emb.1, pred[]{:T(512)S(6)} %eq.12, bf16[1,256,3072]{2,1,0:T(8,128)(2,1)} %param.6), kind=kLoop, calls=%fused_computation.1 | loop fusion | flops 3931648 | bytes 3147777 | tf_op jit(solution)/shard_map/reduce_sum | solution.py:183
  2.2 2.8 %collective-permute-start = (f32[1,3584]{1,0:T(1,128)S(1)}, f32[1,3584]{1,0:T(1,128)S(1)}, u32[]{:S(2)}, u32[]{:S(2)}) collective-permute-start(f32[1,3584]{1,0:T(1,128)S(1)} %pad_maximum_fusion), channel_id=1, source_target_pairs={{0,9},{1,8},{2,11},{3,10},{4,13},{5,12},{6,15},{7,14},{8,1},{9,0},... | collective-permute-start | bytes 43016 | tf_op jit(solution)/shard_map/ppermute | solution.py:43
  5.0 1.1 %collective-permute-done = f32[1,3584]{1,0:T(1,128)S(1)} collective-permute-done((f32[1,3584]{1,0:T(1,128)S(1)}, f32[1,3584]{1,0:T(1,128)S(1)}, u32[]{:S(2)}, u32[]{:S(2)}) %collective-permute-start) | collective-permute-done | bytes 14368 | tf_op jit(solution)/shard_map/ppermute | solution.py:43
  6.3 3.6 %cut.1 = (bf16[256,768]{1,0:T(8,128)(2,1)}, bf16[256,768]{1,0:T(8,128)(2,1)}, bf16[256,768]{1,0:T(8,128)(2,1)}, bf16[256,768]{1,0:T(8,128)(2,1)}, bf16[256,768]{...) custom-call(bf16[256,3072]{1,0:T(8,128)(2,1)} %emb.1, ...), custom_call_target="tpu_custom_call" | custom-call | tf_op jit(solution)/shard_map/cut/pallas_call | solution.py:74
  9.9 2.8 %collective-permute-start.8 = (bf16[256,768]{1,0:T(8,128)(2,1)}, bf16[256,768]{1,0:T(8,128)(2,1)S(1)}, u32[]{:S(2)}, u32[]{:S(2)}) collective-permute-start(bf16[256,768]{1,0:T(8,128)(2,1)} %get-tuple-element.16), channel_id=1, source_target_pairs={{0,9},{1,8},{2,11},{3,10},{4,13},{5,12},{6,15},{7,14},{8,1},{9,0},... | collective-permute-start | bytes 1179656 | tf_op jit(solution)/shard_map/ppermute | solution.py:43
  12.8 3.6 %collective-permute-start.14 = (bf16[256,768]{1,0:T(8,128)(2,1)}, bf16[256,768]{1,0:T(8,128)(2,1)S(1)}, u32[]{:S(2)}, u32[]{:S(2)}) collective-permute-start(bf16[256,768]{1,0:T(8,128)(2,1)} %get-tuple-element.18), channel_id=1, source_target_pairs={{0,242},{1,19},{2,244},{3,21},{4,246},{5,23},{6,240},{7,17},{8,250... | collective-permute-start | bytes 1179656 | tf_op jit(solution)/shard_map/ppermute | solution.py:43
  16.4 1.4 %collective-permute-start.13 = (bf16[256,768]{1,0:T(8,128)(2,1)}, bf16[256,768]{1,0:T(8,128)(2,1)S(1)}, u32[]{:S(2)}, u32[]{:S(2)}) collective-permute-start(bf16[256,768]{1,0:T(8,128)(2,1)} %get-tuple-element.17), channel_id=1, source_target_pairs={{0,18},{1,243},{2,20},{3,245},{4,22},{5,247},{6,16},{7,241},{8,26}... | collective-permute-start | bytes 1179656 | tf_op jit(solution)/shard_map/ppermute | solution.py:43
  17.8 2.5 %collective-permute-start.19 = (bf16[256,768]{1,0:T(8,128)(2,1)}, bf16[256,768]{1,0:T(8,128)(2,1)S(1)}, u32[]{:S(2)}, u32[]{:S(2)}) collective-permute-start(bf16[256,768]{1,0:T(8,128)(2,1)} %get-tuple-element.20), channel_id=1, source_target_pairs={{0,246},{1,23},{2,240},{3,17},{4,242},{5,19},{6,244},{7,21},{8,254... | collective-permute-start | bytes 1179656 | tf_op jit(solution)/shard_map/ppermute | solution.py:43
  20.3 8.3 %collective-permute-start.2 = (f32[2,2,256]{2,1,0:T(2,128)S(1)}, f32[2,2,256]{2,1,0:T(2,128)S(1)}, u32[]{:S(2)}, u32[]{:S(2)}) collective-permute-start(f32[2,2,256]{2,1,0:T(2,128)S(1)} %reverse_select_fusion), channel_id=1, source_target_pairs={{0,20},{1,245},{2,22},{3,247},{4,16},{5,241},{6,18},{7,243},{8,28}... | collective-permute-start | bytes 12296 | tf_op jit(solution)/shard_map/ppermute | solution.py:43
  28.6 1.1 %broadcast_select_fusion.3 = (bf16[256,768]{1,0:T(8,128)(2,1)S(1)}, bf16[256,768]{1,0:T(8,128)(2,1)S(1)}) fusion(bf16[256,768]{1,0:T(8,128)(2,1)S(1)} %collective-permute-done.8, bf16[256,768]{1,0:T(8,128)(2,1)} %get-tuple-element.15, pred[]{:T(512)S(6)} %eq.13), kind=kLoop, calls=%fused_computation.6 | loop fusion | flops 393216 | bytes 1572865 | tf_op jit(solution)/shard_map/jit(_where)/select_n | solution.py:197
  29.8 3.2 %collective-permute-start.7 = (f32[2,2,256]{2,1,0:T(2,128)S(1)}, f32[2,2,256]{2,1,0:T(2,128)S(1)}, u32[]{:S(2)}, u32[]{:S(2)}) collective-permute-start(f32[2,2,256]{2,1,0:T(2,128)S(1)} %reverse_select_fusion), channel_id=1, source_target_pairs={{0,16},{1,241},{2,18},{3,243},{4,20},{5,245},{6,22},{7,247},{8,24}... | collective-permute-start | bytes 12296 | tf_op jit(solution)/shard_map/ppermute | solution.py:43
  34.2 0.8 broadcast_select_fusion.5
  35.0 2.8 %collective-permute-start.18 = (bf16[256,768]{1,0:T(8,128)(2,1)S(1)}, bf16[256,768]{1,0:T(8,128)(2,1)S(1)}, u32[]{:S(2)}, u32[]{:S(2)}) collective-permute-start(bf16[256,768]{1,0:T(8,128)(2,1)S(1)} %copy-done.3), channel_id=1, source_target_pairs={{0,22},{1,247},{2,16},{3,241},{4,18},{5,243},{6,20},{7,245},{8,30}... | collective-permute-start | bytes 1179656 | tf_op jit(solution)/shard_map/ppermute | solution.py:43
  37.8 0.7 collective-permute-start.10
  38.5 0.7 collective-permute-start.5
  39.3 4.1 %collective-permute-start.20 = (bf16[256,768]{1,0:T(8,128)(2,1)S(1)}, bf16[256,768]{1,0:T(8,128)(2,1)S(1)}, u32[]{:S(2)}, u32[]{:S(2)}) collective-permute-start(bf16[256,768]{1,0:T(8,128)(2,1)S(1)} %collective-permute-done.19), channel_id=1, source_target_pairs={{0,9},{1,8},{2,11},{3,10},{4,13},{5,12},{6,15},{7,14},{8,1},{9,0},... | collective-permute-start | bytes 1179656 | tf_op jit(solution)/shard_map/ppermute | solution.py:43
  43.6 6.0 %collective-permute-start.9 = (bf16[256,768]{1,0:T(8,128)(2,1)S(1)}, bf16[256,768]{1,0:T(8,128)(2,1)S(1)}, u32[]{:S(2)}, u32[]{:S(2)}) collective-permute-start(bf16[256,768]{1,0:T(8,128)(2,1)S(1)} %get-tuple-element.24), channel_id=1, source_target_pairs={{0,16},{1,241},{2,18},{3,243},{4,20},{5,245},{6,22},{7,247},{8,24}... | collective-permute-start | bytes 1179656 | tf_op jit(solution)/shard_map/ppermute | solution.py:43
  49.6 0.8 broadcast_select_fusion.2
  50.5 1.3 %collective-permute-start.4 = (bf16[256,768]{1,0:T(8,128)(2,1)}, bf16[256,768]{1,0:T(8,128)(2,1)S(1)}, u32[]{:S(2)}, u32[]{:S(2)}) collective-permute-start(bf16[256,768]{1,0:T(8,128)(2,1)} %get-tuple-element.26), channel_id=1, source_target_pairs={{0,20},{1,245},{2,22},{3,247},{4,16},{5,241},{6,18},{7,243},{8,28}... | collective-permute-start | bytes 1179656 | tf_op jit(solution)/shard_map/ppermute | solution.py:43
  51.8 3.5 %collective-permute-done.5 = bf16[256,768]{1,0:T(8,128)(2,1)} collective-permute-done((bf16[256,768]{1,0:T(8,128)(2,1)S(1)}, bf16[256,768]{1,0:T(8,128)(2,1)}, u32[]{:S(2)}, u32[]{:S(2)}) %collective-permute-start.5) | collective-permute-done | bytes 393248 | tf_op jit(solution)/shard_map/ppermute | solution.py:43
  55.3 6.1 %collective-permute-start.11 = (bf16[256,768]{1,0:T(8,128)(2,1)}, bf16[256,768]{1,0:T(8,128)(2,1)S(1)}, u32[]{:S(2)}, u32[]{:S(2)}) collective-permute-start(bf16[256,768]{1,0:T(8,128)(2,1)} %collective-permute-done.10), channel_id=1, source_target_pairs={{0,16},{1,241},{2,18},{3,243},{4,20},{5,245},{6,22},{7,247},{8,24}... | collective-permute-start | bytes 1179656 | tf_op jit(solution)/shard_map/ppermute | solution.py:43
  61.4 0.8 broadcast_select_fusion.1
  62.2 0.7 slice.8
  62.9 0.7 collective-permute-done.4.k2
  63.6 1.3 %collective-permute-start.12 = (f32[2,2,256]{2,1,0:T(2,128)S(1)}, f32[2,2,256]{2,1,0:T(2,128)S(1)}, u32[]{:S(2)}, u32[]{:S(2)}) collective-permute-start(f32[2,2,256]{2,1,0:T(2,128)S(1)} %reverse_select_fusion), channel_id=1, source_target_pairs={{0,18},{1,243},{2,20},{3,245},{4,22},{5,247},{6,16},{7,241},{8,26}... | collective-permute-start | bytes 12296 | tf_op jit(solution)/shard_map/ppermute | solution.py:43
  64.9 1.5 %collective-permute-done.11.t0 = bf16[256,768]{1,0:T(8,128)(2,1)S(1)} collective-permute-done((bf16[256,768]{1,0:T(8,128)(2,1)}, bf16[256,768]{1,0:T(8,128)(2,1)S(1)}, u32[]{:S(2)}, u32[]{:S(2)}) %collective-permute-start.11) | collective-permute-done | bytes 393248 | tf_op jit(solution)/shard_map/ppermute | solution.py:43
  66.4 1.2 %collective-permute-start.17 = (f32[2,2,256]{2,1,0:T(2,128)S(1)}, f32[2,2,256]{2,1,0:T(2,128)S(1)}, u32[]{:S(2)}, u32[]{:S(2)}) collective-permute-start(f32[2,2,256]{2,1,0:T(2,128)S(1)} %reverse_select_fusion), channel_id=1, source_target_pairs={{0,22},{1,247},{2,16},{3,241},{4,18},{5,243},{6,20},{7,245},{8,30}... | collective-permute-start | bytes 12296 | tf_op jit(solution)/shard_map/ppermute | solution.py:43
  67.7 0.7 broadcast_select_fusion.7.gain
  68.4 6.4 %collective-permute-done.6.t2 = bf16[256,768]{1,0:T(8,128)(2,1)} collective-permute-done((bf16[256,768]{1,0:T(8,128)(2,1)}, bf16[256,768]{1,0:T(8,128)(2,1)}, u32[]{:S(2)}, u32[]{:S(2)}) %collective-permute-start.6) | collective-permute-done | bytes 393248 | tf_op jit(solution)/shard_map/ppermute | solution.py:43
  74.7 3.0 %gram20.1.acc = f32[768,768]{1,0:T(8,128)S(1)} custom-call(f32[1,768]{1,0:T(1,128)S(1)} %broadcast_select_fusion.7.gain, f32[2,2,256]{2,1,0:T(2,128)S(1)} %collective-permute-done.2.sums2, bf16[256,768]{1,0:T(8,128)(2,1)S(1)} %collective-permute-done.4.k2, bf16[256,768]{1,0:T(8,128)(2,1)} %collective-permute-done.6.t2, ...), custom_call_target="tpu_custom_call" | custom-call | tf_op jit(solution)/shard_map/gram20/pallas_call | solution.py:157
  77.8 1.3 %gram1.1.acc = f32[768,768]{1,0:T(8,128)S(1)} custom-call(f32[768,768]{1,0:T(8,128)S(1)} %gram20.1.acc, f32[1,768]{1,0:T(1,128)S(1)} %broadcast_select_fusion.7.gain, f32[2,2,256]{2,1,0:T(2,128)S(1)} %collective-permute-done.12.sums, bf16[256,768]{1,0:T(8,128)(2,1)S(1)} %collective-permute-done.13.b, bf16[256,768]{1,0:T(8,128)(2,1)S(1)} %collective-permute-done.15.a, ...), custom_call_target="tpu_custom_call" | custom-call | tf_op jit(solution)/shard_map/gram1/pallas_call | solution.py:157
  79.1 19.3 %gram3.1 = f32[768,768]{1,0:T(8,128)} custom-call(f32[768,768]{1,0:T(8,128)S(1)} %gram1.1.acc, f32[1,768]{1,0:T(1,128)S(1)} %broadcast_select_fusion.7.gain, f32[2,2,256]{2,1,0:T(2,128)S(1)} %collective-permute-done.17.sums, bf16[256,768]{1,0:T(8,128)(2,1)S(1)} %collective-permute-done.18.b, bf16[256,768]{1,0:T(8,128)(2,1)S(1)} %collective-permute-done.20.a, ...), custom_call_target="tpu_custom_call" | custom-call | tf_op jit(solution)/shard_map/gram3/pallas_call | solution.py:157
  (39 shorter events, 2.0 us)
Async XLA Ops:
  0.0 2.2 %copy-start.1 = (f32[1,3072]{1,0:T(1,128)S(1)}, f32[1,3072]{1,0:T(1,128)}, u32[]{:S(2)}) copy-start(f32[1,3072]{1,0:T(1,128)} %param.7) | copy-start | bytes 36868
  2.2 3.9 %collective-permute-start = (f32[1,3584]{1,0:T(1,128)S(1)}, f32[1,3584]{1,0:T(1,128)S(1)}, u32[]{:S(2)}, u32[]{:S(2)}) collective-permute-start(f32[1,3584]{1,0:T(1,128)S(1)} %pad_maximum_fusion), channel_id=1, source_target_pairs={{0,9},{1,8},{2,11},{3,10},{4,13},{5,12},{6,15},{7,14},{8,1},{9,0},... | collective-permute-start | bytes 43016 | tf_op jit(solution)/shard_map/ppermute | solution.py:43
  6.1 3.7 %copy-start.2 = (f32[1,3584]{1,0:T(1,128)}, f32[1,3584]{1,0:T(1,128)S(1)}, u32[]{:S(2)}) copy-start(f32[1,3584]{1,0:T(1,128)S(1)} %collective-permute-done) | copy-start | bytes 43012
  6.2 11.6 %collective-permute-start.1 = (f32[2,2,256]{2,1,0:T(2,128)S(1)}, f32[2,2,256]{2,1,0:T(2,128)S(1)}, u32[]{:S(2)}, u32[]{:S(2)}) collective-permute-start(f32[2,2,256]{2,1,0:T(2,128)S(1)} %pad_maximum_fusion.1), channel_id=1, source_target_pairs={{0,8},{1,9},{2,10},{3,11},{4,12},{5,13},{6,14},{7,15},{8,0},{9,1},... | collective-permute-start | bytes 12296 | tf_op jit(solution)/shard_map/ppermute | solution.py:43
  9.9 24.3 %copy-start = (bf16[256,768]{1,0:T(8,128)(2,1)S(1)}, bf16[256,768]{1,0:T(8,128)(2,1)}, u32[]{:S(2)}) copy-start(bf16[256,768]{1,0:T(8,128)(2,1)} %get-tuple-element.13) | copy-start | bytes 1179652
  9.9 10.4 %collective-permute-start.8 = (bf16[256,768]{1,0:T(8,128)(2,1)}, bf16[256,768]{1,0:T(8,128)(2,1)S(1)}, u32[]{:S(2)}, u32[]{:S(2)}) collective-permute-start(bf16[256,768]{1,0:T(8,128)(2,1)} %get-tuple-element.16), channel_id=1, source_target_pairs={{0,9},{1,8},{2,11},{3,10},{4,13},{5,12},{6,15},{7,14},{8,1},{9,0},... | collective-permute-start | bytes 1179656 | tf_op jit(solution)/shard_map/ppermute | solution.py:43
  12.7 17.1 %collective-permute-start.3 = (bf16[256,768]{1,0:T(8,128)(2,1)}, bf16[256,768]{1,0:T(8,128)(2,1)S(1)}, u32[]{:S(2)}, u32[]{:S(2)}) collective-permute-start(bf16[256,768]{1,0:T(8,128)(2,1)} %get-tuple-element.14), channel_id=1, source_target_pairs={{0,9},{1,8},{2,11},{3,10},{4,13},{5,12},{6,15},{7,14},{8,1},{9,0},... | collective-permute-start | bytes 1179656 | tf_op jit(solution)/shard_map/ppermute | solution.py:43
  12.8 20.7 %collective-permute-start.14 = (bf16[256,768]{1,0:T(8,128)(2,1)}, bf16[256,768]{1,0:T(8,128)(2,1)S(1)}, u32[]{:S(2)}, u32[]{:S(2)}) collective-permute-start(bf16[256,768]{1,0:T(8,128)(2,1)} %get-tuple-element.18), channel_id=1, source_target_pairs={{0,242},{1,19},{2,244},{3,21},{4,246},{5,23},{6,240},{7,17},{8,250... | collective-permute-start | bytes 1179656 | tf_op jit(solution)/shard_map/ppermute | solution.py:43
  16.4 22.1 %collective-permute-start.13 = (bf16[256,768]{1,0:T(8,128)(2,1)}, bf16[256,768]{1,0:T(8,128)(2,1)S(1)}, u32[]{:S(2)}, u32[]{:S(2)}) collective-permute-start(bf16[256,768]{1,0:T(8,128)(2,1)} %get-tuple-element.17), channel_id=1, source_target_pairs={{0,18},{1,243},{2,20},{3,245},{4,22},{5,247},{6,16},{7,241},{8,26}... | collective-permute-start | bytes 1179656 | tf_op jit(solution)/shard_map/ppermute | solution.py:43
  17.8 21.5 %collective-permute-start.19 = (bf16[256,768]{1,0:T(8,128)(2,1)}, bf16[256,768]{1,0:T(8,128)(2,1)S(1)}, u32[]{:S(2)}, u32[]{:S(2)}) collective-permute-start(bf16[256,768]{1,0:T(8,128)(2,1)} %get-tuple-element.20), channel_id=1, source_target_pairs={{0,246},{1,23},{2,240},{3,17},{4,242},{5,19},{6,244},{7,21},{8,254... | collective-permute-start | bytes 1179656 | tf_op jit(solution)/shard_map/ppermute | solution.py:43
  20.3 14.7 %collective-permute-start.2 = (f32[2,2,256]{2,1,0:T(2,128)S(1)}, f32[2,2,256]{2,1,0:T(2,128)S(1)}, u32[]{:S(2)}, u32[]{:S(2)}) collective-permute-start(f32[2,2,256]{2,1,0:T(2,128)S(1)} %reverse_select_fusion), channel_id=1, source_target_pairs={{0,20},{1,245},{2,22},{3,247},{4,16},{5,241},{6,18},{7,243},{8,28}... | collective-permute-start | bytes 12296 | tf_op jit(solution)/shard_map/ppermute | solution.py:43
  28.6 6.4 %copy-start.3 = (bf16[256,768]{1,0:T(8,128)(2,1)S(1)}, bf16[256,768]{1,0:T(8,128)(2,1)}, u32[]{:S(2)}) copy-start(bf16[256,768]{1,0:T(8,128)(2,1)} %get-tuple-element.19) | copy-start | bytes 1179652
  29.8 8.0 %collective-permute-start.7 = (f32[2,2,256]{2,1,0:T(2,128)S(1)}, f32[2,2,256]{2,1,0:T(2,128)S(1)}, u32[]{:S(2)}, u32[]{:S(2)}) collective-permute-start(f32[2,2,256]{2,1,0:T(2,128)S(1)} %reverse_select_fusion), channel_id=1, source_target_pairs={{0,16},{1,241},{2,18},{3,243},{4,20},{5,245},{6,22},{7,247},{8,24}... | collective-permute-start | bytes 12296 | tf_op jit(solution)/shard_map/ppermute | solution.py:43
  33.5 10.1 %collective-permute-start.15 = (bf16[256,768]{1,0:T(8,128)(2,1)S(1)}, bf16[256,768]{1,0:T(8,128)(2,1)S(1)}, u32[]{:S(2)}, u32[]{:S(2)}) collective-permute-start(bf16[256,768]{1,0:T(8,128)(2,1)S(1)} %collective-permute-done.14), channel_id=1, source_target_pairs={{0,9},{1,8},{2,11},{3,10},{4,13},{5,12},{6,15},{7,14},{8,1},{9,0},... | collective-permute-start | bytes 1179656 | tf_op jit(solution)/shard_map/ppermute | solution.py:43
  35.0 15.5 %collective-permute-start.18 = (bf16[256,768]{1,0:T(8,128)(2,1)S(1)}, bf16[256,768]{1,0:T(8,128)(2,1)S(1)}, u32[]{:S(2)}, u32[]{:S(2)}) collective-permute-start(bf16[256,768]{1,0:T(8,128)(2,1)S(1)} %copy-done.3), channel_id=1, source_target_pairs={{0,22},{1,247},{2,16},{3,241},{4,18},{5,243},{6,20},{7,245},{8,30}... | collective-permute-start | bytes 1179656 | tf_op jit(solution)/shard_map/ppermute | solution.py:43
  37.8 14.0 %collective-permute-start.10 = (bf16[256,768]{1,0:T(8,128)(2,1)S(1)}, bf16[256,768]{1,0:T(8,128)(2,1)}, u32[]{:S(2)}, u32[]{:S(2)}) collective-permute-start(bf16[256,768]{1,0:T(8,128)(2,1)S(1)} %get-tuple-element.23), channel_id=1, source_target_pairs={{0,8},{1,9},{2,10},{3,11},{4,12},{5,13},{6,14},{7,15},{8,0},{9,1},... | collective-permute-start | bytes 1179656 | tf_op jit(solution)/shard_map/ppermute | solution.py:43
  38.5 16.8 %collective-permute-start.5 = (bf16[256,768]{1,0:T(8,128)(2,1)S(1)}, bf16[256,768]{1,0:T(8,128)(2,1)}, u32[]{:S(2)}, u32[]{:S(2)}) collective-permute-start(bf16[256,768]{1,0:T(8,128)(2,1)S(1)} %get-tuple-element.25), channel_id=1, source_target_pairs={{0,8},{1,9},{2,10},{3,11},{4,12},{5,13},{6,14},{7,15},{8,0},{9,1},... | collective-permute-start | bytes 1179656 | tf_op jit(solution)/shard_map/ppermute | solution.py:43
  39.3 22.1 %collective-permute-start.20 = (bf16[256,768]{1,0:T(8,128)(2,1)S(1)}, bf16[256,768]{1,0:T(8,128)(2,1)S(1)}, u32[]{:S(2)}, u32[]{:S(2)}) collective-permute-start(bf16[256,768]{1,0:T(8,128)(2,1)S(1)} %collective-permute-done.19), channel_id=1, source_target_pairs={{0,9},{1,8},{2,11},{3,10},{4,13},{5,12},{6,15},{7,14},{8,1},{9,0},... | collective-permute-start | bytes 1179656 | tf_op jit(solution)/shard_map/ppermute | solution.py:43
  43.6 18.6 %collective-permute-start.9 = (bf16[256,768]{1,0:T(8,128)(2,1)S(1)}, bf16[256,768]{1,0:T(8,128)(2,1)S(1)}, u32[]{:S(2)}, u32[]{:S(2)}) collective-permute-start(bf16[256,768]{1,0:T(8,128)(2,1)S(1)} %get-tuple-element.24), channel_id=1, source_target_pairs={{0,16},{1,241},{2,18},{3,243},{4,20},{5,245},{6,22},{7,247},{8,24}... | collective-permute-start | bytes 1179656 | tf_op jit(solution)/shard_map/ppermute | solution.py:43
  50.5 13.1 %collective-permute-start.4 = (bf16[256,768]{1,0:T(8,128)(2,1)}, bf16[256,768]{1,0:T(8,128)(2,1)S(1)}, u32[]{:S(2)}, u32[]{:S(2)}) collective-permute-start(bf16[256,768]{1,0:T(8,128)(2,1)} %get-tuple-element.26), channel_id=1, source_target_pairs={{0,20},{1,245},{2,22},{3,247},{4,16},{5,241},{6,18},{7,243},{8,28}... | collective-permute-start | bytes 1179656 | tf_op jit(solution)/shard_map/ppermute | solution.py:43
  51.8 25.9 %collective-permute-start.16 = (bf16[256,768]{1,0:T(8,128)(2,1)}, bf16[256,768]{1,0:T(8,128)(2,1)S(1)}, u32[]{:S(2)}, u32[]{:S(2)}) collective-permute-start(bf16[256,768]{1,0:T(8,128)(2,1)} %broadcast_select_fusion.2), channel_id=1, source_target_pairs={{0,8},{1,9},{2,10},{3,11},{4,12},{5,13},{6,14},{7,15},{8,0},{9,1},... | collective-permute-start | bytes 1179656 | tf_op jit(solution)/shard_map/ppermute | solution.py:43
  55.3 11.1 %collective-permute-start.11 = (bf16[256,768]{1,0:T(8,128)(2,1)}, bf16[256,768]{1,0:T(8,128)(2,1)S(1)}, u32[]{:S(2)}, u32[]{:S(2)}) collective-permute-start(bf16[256,768]{1,0:T(8,128)(2,1)} %collective-permute-done.10), channel_id=1, source_target_pairs={{0,16},{1,241},{2,18},{3,243},{4,20},{5,245},{6,22},{7,247},{8,24}... | collective-permute-start | bytes 1179656 | tf_op jit(solution)/shard_map/ppermute | solution.py:43
  61.4 13.3 %collective-permute-start.6 = (bf16[256,768]{1,0:T(8,128)(2,1)}, bf16[256,768]{1,0:T(8,128)(2,1)}, u32[]{:S(2)}, u32[]{:S(2)}) collective-permute-start(bf16[256,768]{1,0:T(8,128)(2,1)} %collective-permute-done.5), channel_id=1, source_target_pairs={{0,20},{1,245},{2,22},{3,247},{4,16},{5,241},{6,18},{7,243},{8,28}... | collective-permute-start | bytes 1179656 | tf_op jit(solution)/shard_map/ppermute | solution.py:43
  62.2 16.9 %collective-permute-start.21 = (bf16[256,768]{1,0:T(8,128)(2,1)}, bf16[256,768]{1,0:T(8,128)(2,1)S(1)}, u32[]{:S(2)}, u32[]{:S(2)}) collective-permute-start(bf16[256,768]{1,0:T(8,128)(2,1)} %broadcast_select_fusion.1), channel_id=1, source_target_pairs={{0,8},{1,9},{2,10},{3,11},{4,12},{5,13},{6,14},{7,15},{8,0},{9,1},... | collective-permute-start | bytes 1179656 | tf_op jit(solution)/shard_map/ppermute | solution.py:43
  63.6 14.2 %collective-permute-start.12 = (f32[2,2,256]{2,1,0:T(2,128)S(1)}, f32[2,2,256]{2,1,0:T(2,128)S(1)}, u32[]{:S(2)}, u32[]{:S(2)}) collective-permute-start(f32[2,2,256]{2,1,0:T(2,128)S(1)} %reverse_select_fusion), channel_id=1, source_target_pairs={{0,18},{1,243},{2,20},{3,245},{4,22},{5,247},{6,16},{7,241},{8,26}... | collective-permute-start | bytes 12296 | tf_op jit(solution)/shard_map/ppermute | solution.py:43
  66.4 12.7 %collective-permute-start.17 = (f32[2,2,256]{2,1,0:T(2,128)S(1)}, f32[2,2,256]{2,1,0:T(2,128)S(1)}, u32[]{:S(2)}, u32[]{:S(2)}) collective-permute-start(f32[2,2,256]{2,1,0:T(2,128)S(1)} %reverse_select_fusion), channel_id=1, source_target_pairs={{0,22},{1,247},{2,16},{3,241},{4,18},{5,243},{6,20},{7,245},{8,30}... | collective-permute-start | bytes 12296 | tf_op jit(solution)/shard_map/ppermute | solution.py:43

commit v3 on v2

v3 whole, which is shorter than its diff:
```python
import functools

import jax
import jax.numpy as jnp
from jax import lax
from jax.experimental import pallas as pl
from jax.experimental.pallas import tpu as pltpu
from jax.sharding import PartitionSpec as P

D = 6144
BLK = 768
TOKENS = 2048
SECTIONS, REPLICAS, HALVES = 16, 8, 2
ROWS = TOKENS // REPLICAS
COLS = D // HALVES
EXTRA = 16
AXES = ("section", "dp", "tensor")


def pairs(move):
    out = []
    for s in range(SECTIONS):
        for d in range(REPLICAS):
            for h in range(HALVES):
                to_s, x, y = move(s, d % 4, 2 * h + d // 4)
                to = ((to_s % SECTIONS) * REPLICAS + (y % 2) * 4 + x % 4) * HALVES + y // 2
                out.append(((s * REPLICAS + d) * HALVES + h, to))
    return out


def across(shift, own):
    def move(s, x, y):
        kind = y // 2 if own else 1 - y // 2
        return (s + 1 if kind == 0 else s - 1), x + shift, y

    return pairs(move)


SIGMA = pairs(lambda s, x, y: (s, x, y ^ 3))
TAU = pairs(lambda s, x, y: (s, x, y ^ 1))


CUTS = [(own, shift) for own in (False, True) for shift in range(4)]


def send(name, block, route, *after):
    with jax.named_scope(name):
        if after:
            block = lax.optimization_barrier((block, *after))[0]
        return lax.ppermute(block, AXES, route)


def coded(rows):
    parts = []
    for _ in range(3):
        parts.append(rows.astype(jnp.bfloat16))
        rows = rows - parts[-1].astype(jnp.float32)
    return jnp.concatenate(parts, axis=1)


def decoded(block):
    block = block.astype(jnp.float32)
    return block[:, :ROWS] + block[:, ROWS : 2 * ROWS] + block[:, 2 * ROWS :]


PARTS = 4


def cut_kernel(emb, outs, grads, loss, *rest):
    chunks, (hidden, grad, tail, in_sems, out_sems, tail_sems) = rest[:-6], rest[-6:]
    s = lax.axis_index("section")
    x = lax.rem(lax.axis_index("dp"), 4)
    h = lax.axis_index("tensor")
    step = ROWS // PARTS

    def load(source, target, part, sem):
        rows = pl.ds(part * step, step)
        return pltpu.make_async_copy(source.at[rows], target.at[rows], in_sems.at[sem + part])

    for edge in (True, False):
        for section, source, target, sem in (
            (SECTIONS - 1, emb if edge else outs, hidden, 0),
            (0, loss if edge else grads, grad, PARTS),
        ):
            @pl.when((s == section) == edge)
            def _():
                for part in range(PARTS):
                    load(source, target, part, sem).start()

    for part in range(PARTS):
        load(outs, hidden, part, 0).wait()
    for part in range(PARTS):
        load(grads, grad, part, PARTS).wait()

    def store(r, source):
        cols = pl.ds(pl.multiple_of(lax.rem(x + CUTS[r][1], 4) * BLK, BLK), BLK)
        return pltpu.make_async_copy(source.at[:, cols], chunks[r].at[:ROWS], out_sems.at[r])

    for r, (own, _) in enumerate(CUTS):
        for kind, source in ((0, hidden), (1, grad)):
            @pl.when((h == kind) == own)
            def _():
                store(r, source).start()

    values = hidden[...].astype(jnp.float32)
    total = jnp.sum(values, axis=1, keepdims=True)
    power = jnp.sum(values * values, axis=1, keepdims=True)
    odd = lax.broadcasted_iota(jnp.int32, (ROWS, 128), 1) % 2 == 1
    tail[...] = coded(jnp.where(odd, power, total).T[:EXTRA, :])
    tails = [
        pltpu.make_async_copy(tail, chunk.at[ROWS:], tail_sems.at[r])
        for r, chunk in enumerate(chunks)
    ]
    for copy in tails:
        copy.start()
    for r in range(len(CUTS)):
        store(r, hidden).wait()
    for copy in tails:
        copy.wait()


def cut(emb, outs, grads, loss):
    any_spec = pl.BlockSpec(memory_space=pl.ANY)
    return pl.pallas_call(
        cut_kernel,
        out_shape=[jax.ShapeDtypeStruct((ROWS + EXTRA, BLK), jnp.bfloat16)] * len(CUTS),
        in_specs=[any_spec] * 4,
        out_specs=[any_spec] * len(CUTS),
        scratch_shapes=[
            pltpu.VMEM((ROWS, COLS), jnp.bfloat16),
            pltpu.VMEM((ROWS, COLS), jnp.bfloat16),
            pltpu.VMEM((EXTRA, BLK), jnp.bfloat16),
            pltpu.SemaphoreType.DMA((2 * PARTS,)),
            pltpu.SemaphoreType.DMA((len(CUTS),)),
            pltpu.SemaphoreType.DMA((len(CUTS),)),
        ],
        name="cut",
    )(emb, outs, grads, loss)


def relay_kernel(a, b, onward, *kept):
    keeper = keeps()
    onward[:ROWS, :] = jnp.where(keeper, a[:ROWS, :], b[:ROWS, :])
    crossed = lax.broadcasted_iota(jnp.int32, (EXTRA, BLK), 0) % 4 >= 2
    onward[ROWS:, :] = jnp.where(crossed, a[ROWS:, :], b[ROWS:, :])
    for out in kept:
        out[...] = jnp.where(keeper, b[:ROWS, :], a[:ROWS, :])


def relay(a, b, with_kept=False):
    vmem = pl.BlockSpec(memory_space=pltpu.VMEM)
    shapes = [jax.ShapeDtypeStruct((rows, BLK), jnp.bfloat16) for rows in (ROWS + EXTRA, ROWS)]
    shapes = shapes[: 1 + with_kept]
    return pl.pallas_call(
        relay_kernel,
        out_shape=shapes,
        in_specs=[vmem] * 2,
        out_specs=[vmem] * len(shapes),
        compiler_params=pltpu.CompilerParams(vmem_limit_bytes=4 * 2**20),
        name="relay",
    )(a, b)


def forward_kernel(t, own, out):
    out[:ROWS, :] = t[:ROWS, :]
    first = lax.broadcasted_iota(jnp.int32, (EXTRA, BLK), 0) < 4
    out[ROWS:, :] = jnp.where(first, t[ROWS:, :], own[ROWS:, :])


def forward(t, own):
    vmem = pl.BlockSpec(memory_space=pltpu.VMEM)
    return pl.pallas_call(
        forward_kernel,
        out_shape=jax.ShapeDtypeStruct(t.shape, t.dtype),
        in_specs=[vmem] * 2,
        out_specs=vmem,
        compiler_params=pltpu.CompilerParams(vmem_limit_bytes=4 * 2**20),
        name="forward",
    )(t, own)


def gain_columns(gain, other):
    d = lax.axis_index("dp")
    x, first_half = lax.rem(d, 4), lax.div(d, 4) == 0
    cols = pl.ds(pl.multiple_of(x * BLK, BLK), BLK)
    return jnp.where(first_half, gain[:, cols], other[:, cols])


def pair_rows(first, second, mine, crossed, beside, relayed, gain_row):
    is_input = lax.axis_index("tensor") == 0
    same, swapped = mine + relayed, crossed + beside
    stats = jnp.concatenate(
        [jnp.where(keeps(), same, swapped), jnp.where(keeps(), swapped, same)] * 2, axis=0
    ).T / D
    gain = jnp.where(is_input, gain_row, 1.0)
    rows = []
    for chunk, c in ((first, 0), (second, 2)):
        mean, power = stats[:, c : c + 1], stats[:, c + 1 : c + 2]
        scale = jnp.where(is_input, lax.rsqrt(power - mean * mean + 1e-05), 1.0)
        mean = jnp.where(is_input, mean, 0.0)
        rows.append(((chunk.astype(jnp.float32) - mean) * scale * gain).astype(jnp.bfloat16))
    return rows


def gram(rows):
    rows = jnp.concatenate(rows, axis=0)
    return lax.dot_general(
        rows, rows, (((0,), (0,)), ((), ())), preferred_element_type=jnp.float32
    )


def keeps():
    return lax.axis_index("tensor") == lax.div(lax.axis_index("dp"), 4)


def early_rows(b, a, t, row):
    mine, crossed, rest = (decoded(r[ROWS:, :]) for r in (b, a, t))
    kept = jnp.where(keeps(), b[:ROWS, :], a[:ROWS, :])
    return pair_rows(kept, t[:ROWS, :], mine[:2], crossed[:2], rest[:2], rest[2:4], row)


def late_rows(k, t, row):
    rest = decoded(t[ROWS:, :])
    return pair_rows(k[...], t[:ROWS, :], rest[4:6], rest[6:8], rest[:2], rest[2:4], row)


def early_kernel(gain, other, b1, a1, t1, k0, t0, out):
    row = gain_columns(gain, other)
    out[...] = gram(early_rows(b1, a1, t1, row) + late_rows(k0, t0, row))


def split(a):
    hi = a.astype(jnp.bfloat16)
    return hi, (a - hi.astype(jnp.float32)).astype(jnp.bfloat16)


TILE = 256
STRIPES = [(slice(0, j + TILE), slice(j, j + TILE)) for j in range(0, BLK, TILE)]


def product(a, b, rows, cols):
    def dot(p, q):
        return jnp.dot(p[rows, :], q[:, cols], preferred_element_type=jnp.float32)

    return dot(a[0], b[0]) + dot(a[0], b[1]) + dot(a[1], b[0])


def put_symmetric(parts, rows, cols, value):
    for ref, part in zip(parts, split(value)):
        ref[rows, cols] = part
    if cols.start:
        above = slice(0, cols.start)
        for ref, part in zip(parts, split(value[above, :].T)):
            ref[cols, above] = part


def invert(total, out, first, second, fourth, low_parts, low, whole, sems):
    row = lax.broadcasted_iota(jnp.int32, (BLK, BLK), 0)
    col = lax.broadcasted_iota(jnp.int32, (BLK, BLK), 1)
    eye = jnp.where(row == col, 1.0, 0.0).astype(jnp.float32)
    damped = total * (1.0 / TOKENS) + 0.05 * eye
    bound = jnp.max(jnp.sum(jnp.abs(damped), axis=0, keepdims=True))
    inverse_bound = 1.0 / bound
    error = eye - damped * inverse_bound
    first[0][...], first[1][...] = split(error)
    low[...] = eye + error
    for rows, cols in STRIPES:
        value = product(first, first, rows, cols)
        put_symmetric(second, rows, cols, value)
        low[rows, cols] += value
    for rows, cols in STRIPES:
        value = low[rows, cols] + product(first, second, rows, cols)
        low[rows, cols] = value
        put_symmetric(low_parts, rows, cols, value)
        put_symmetric(fourth, rows, cols, product(second, second, rows, cols))
    copies = []
    for rows, cols in reversed(STRIPES):
        value = (low[rows, cols] + product(low_parts, fourth, rows, cols)) * inverse_bound
        whole[rows, cols] = value
        if cols.start:
            whole[cols, : cols.start] = value[: cols.start, :].T
        copies.append(pltpu.make_async_copy(whole.at[cols], out.at[cols], sems.at[len(copies)]))
        copies[-1].start()
    for copy in copies:
        copy.wait()


def last_kernel(acc, gain, other, b3, a3, t3, k2, t2, out, *scratch):
    row = gain_columns(gain, other)
    total = acc[...] + gram(early_rows(b3, a3, t3, row) + late_rows(k2, t2, row))
    pairs_of = [scratch[i : i + 2] for i in range(0, 8, 2)]
    invert(total, out, *pairs_of, *scratch[8:])


def in_vmem(kernel, name, args, out_space=pltpu.VMEM, scratch=()):
    vmem = pl.BlockSpec(memory_space=pltpu.VMEM)
    return pl.pallas_call(
        kernel,
        out_shape=jax.ShapeDtypeStruct((BLK, BLK), jnp.float32),
        in_specs=[vmem] * len(args),
        out_specs=pl.BlockSpec(memory_space=out_space),
        scratch_shapes=scratch,
        compiler_params=pltpu.CompilerParams(vmem_limit_bytes=32 * 2**20),
        name=name,
    )(*args)


def per_device(embeddings, section_outputs, norm_gain, input_grads, loss_grads):
    a0, a1, a2, a3, b0, b1, b2, b3 = cut(embeddings, section_outputs[0], input_grads[0], loss_grads)
    ra2 = send("sigma2", a2, SIGMA)
    xa1 = send("xa1", a1, across(1, False))
    xa3 = send("xa3", a3, across(3, False))
    ra0 = send("sigma0", a0, SIGMA)
    xb1 = send("xb1", b1, across(1, True))

    t2, k2 = relay(ra2, b2, True)
    rt2 = send("tau2", t2, TAU)
    ra1 = send("sigma1", xa1, SIGMA, ra2)
    xb3 = send("xb3", b3, across(3, True), xa3)
    t0, k0 = relay(ra0, b0, True)
    rt0 = send("tau0", t0, TAU)
    xk2 = send("xk2", k2, across(2, True), xb1)
    ra3 = send("sigma3", xa3, SIGMA, ra0)
    other = send("gain", norm_gain, SIGMA, rt2)
    xk0 = send("xk0", k0, across(0, True), xb3)
    rt1 = send("tau1", *relay(ra1, xb1), TAU, rt2)
    xt0 = send("xt0", forward(rt0, t0), across(0, True))
    xt2 = send("xt2", forward(rt2, t2), across(2, True), xb3, xk2)
    rt3 = send("tau3", *relay(ra3, xb3), TAU, rt0, other, xk0)

    total = in_vmem(early_kernel, "early", (norm_gain, other, xb1, ra1, rt1, xk0, xt0))
    square = (BLK, BLK)
    result = in_vmem(
        last_kernel,
        "last",
        (total, norm_gain, other, xb3, ra3, rt3, xk2, xt2),
        pl.ANY,
        [pltpu.VMEM(square, jnp.bfloat16)] * 8
        + [pltpu.VMEM(square, jnp.float32)] * 2
        + [pltpu.SemaphoreType.DMA((len(STRIPES),))],
    )
    return result.reshape(1, 1, 1, BLK, BLK)


def solution(mesh):
    placed = (
        P("dp", "tensor"),
        P("section", "dp", "tensor"),
        P("section", "tensor"),
        P("section", "dp", "tensor"),
        P("dp", "tensor"),
    )
    return jax.shard_map(
        per_device,
        mesh=mesh,
        in_specs=placed,
        out_specs=P("section", "tensor", "dp", None, None),
        check_vma=False,
    )
```

time: 98.7 us -> 78.4 us (0.79)
  the two profiles are of different devices: /device:TPU:3 before, /device:TPU:1 now
where the time goes in v3:
time: 78.4 us; the launch traced here: 77.8 us
  starting transfers between devices  30.4 us (39%)
  waiting for transfers between devices  26.1 us (33%)
  Pallas kernels  19 us (24%)
  local copies, waits for them, and re-layouts  2.02 us (3%)
    ppermute x17, starting transfers between devices, send(): return lax.ppermute(block, AXES, route)  30.4 us
    ppermute x17, waiting for transfers between devices, send(): return lax.ppermute(block, AXES, route)  26.1 us
    pallas_call x2, Pallas kernels, in_vmem(): pl.pallas_call(kernel, out_shape=jax.ShapeDtypeStruct((BLK, BLK), jnp.flo...  14.9 us
    pallas_call x1, Pallas kernels, cut(): pl.pallas_call(cut_kernel, out_shape=[jax.ShapeDtypeStruct((ROWS + EXTRA,...  3.74 us
    unnamed x6, local copies, waits for them, and re-layouts  2.02 us
  transfers between devices with their start and end apart: 17, of which 6 were waited for; matrix products, arithmetic and copies ran while one was open for 0% of the time, Pallas kernels for 3%

profile of v3, /device:TPU:1, one launch (start us, length us, event | category | flops | bytes accessed | tf_op | source)
XLA Modules:
  0.0 77.8 jit_solution(2394011652875934856)
XLA Ops:
  0.0 3.7 %cut.1 = (bf16[272,768]{1,0:T(8,128)(2,1)}, bf16[272,768]{1,0:T(8,128)(2,1)}, bf16[272,768]{1,0:T(8,128)(2,1)}, bf16[272,768]{1,0:T(8,128)(2,1)}, bf16[272,768]{...) custom-call(bf16[256,3072]{1,0:T(8,128)(2,1)} %emb.1, ...), custom_call_target="tpu_custom_call" | custom-call | tf_op jit(solution)/shard_map/cut/pallas_call | solution.py:124
  3.7 0.0 copy-start.2
  3.8 4.0 %collective-permute-start.8 = (bf16[272,768]{1,0:T(8,128)(2,1)}, bf16[272,768]{1,0:T(8,128)(2,1)S(1)}, u32[]{:S(2)}, u32[]{:S(2)}) collective-permute-start(bf16[272,768]{1,0:T(8,128)(2,1)} %get-tuple-element.38), channel_id=1, source_target_pairs={{0,246},{1,23},{2,240},{3,17},{4,242},{5,19},{6,244},{7,21},{8,254... | collective-permute-start | bytes 1253384 | tf_op jit(solution)/shard_map/xa3/ppermute | solution.py:50
  7.7 4.1 %collective-permute-start = (bf16[272,768]{1,0:T(8,128)(2,1)}, bf16[272,768]{1,0:T(8,128)(2,1)S(1)}, u32[]{:S(2)}, u32[]{:S(2)}) collective-permute-start(bf16[272,768]{1,0:T(8,128)(2,1)} %get-tuple-element.26), channel_id=1, source_target_pairs={{0,9},{1,8},{2,11},{3,10},{4,13},{5,12},{6,15},{7,14},{8,1},{9,0},... | collective-permute-start | bytes 1253384 | tf_op jit(solution)/shard_map/sigma2/ppermute | solution.py:50
  11.8 0.0 collective-permute-start.7
  11.8 2.1 %collective-permute-start.3 = (bf16[272,768]{1,0:T(8,128)(2,1)}, bf16[272,768]{1,0:T(8,128)(2,1)S(1)}, u32[]{:S(2)}, u32[]{:S(2)}) collective-permute-start(bf16[272,768]{1,0:T(8,128)(2,1)} %get-tuple-element.30), channel_id=1, source_target_pairs={{0,18},{1,243},{2,20},{3,245},{4,22},{5,247},{6,16},{7,241},{8,26}... | collective-permute-start | bytes 1253384 | tf_op jit(solution)/shard_map/xb1/ppermute | solution.py:50
  13.9 3.6 %collective-permute-done.8 = bf16[272,768]{1,0:T(8,128)(2,1)S(1)} collective-permute-done((bf16[272,768]{1,0:T(8,128)(2,1)}, bf16[272,768]{1,0:T(8,128)(2,1)S(1)}, u32[]{:S(2)}, u32[]{:S(2)}) %collective-permute-start.8) | collective-permute-done | bytes 417824 | tf_op jit(solution)/shard_map/xa3/ppermute | solution.py:50
  17.5 4.9 %collective-permute-start.9 = (bf16[272,768]{1,0:T(8,128)(2,1)}, bf16[272,768]{1,0:T(8,128)(2,1)S(1)}, u32[]{:S(2)}, u32[]{:S(2)}) collective-permute-start(bf16[272,768]{1,0:T(8,128)(2,1)} %get-tuple-element.39), channel_id=1, source_target_pairs={{0,22},{1,247},{2,16},{3,241},{4,18},{5,243},{6,20},{7,245},{8,30}... | collective-permute-start | bytes 1253384 | tf_op jit(solution)/shard_map/xb3/ppermute | solution.py:50
  22.4 0.0 collective-permute-done.a
  22.4 1.0 %copy-done.1 = bf16[272,768]{1,0:T(8,128)(2,1)S(1)} copy-done((bf16[272,768]{1,0:T(8,128)(2,1)S(1)}, bf16[272,768]{1,0:T(8,128)(2,1)}, u32[]{:S(2)}) %copy-start.1) | copy-done | bytes 417816
  23.4 0.1 relay.4
  23.5 1.4 %collective-permute-start.1 = (bf16[272,768]{1,0:T(8,128)(2,1)S(1)}, bf16[272,768]{1,0:T(8,128)(2,1)S(1)}, u32[]{:S(2)}, u32[]{:S(2)}) collective-permute-start(bf16[272,768]{1,0:T(8,128)(2,1)S(1)} %get-tuple-element.28.own), channel_id=1, source_target_pairs={{0,8},{1,9},{2,10},{3,11},{4,12},{5,13},{6,14},{7,15},{8,0},{9,1},... | collective-permute-start | bytes 1253384 | tf_op jit(solution)/shard_map/tau2/ppermute | solution.py:50
  24.9 4.1 %collective-permute-done.4 = bf16[272,768]{1,0:T(8,128)(2,1)S(1)} collective-permute-done((bf16[272,768]{1,0:T(8,128)(2,1)}, bf16[272,768]{1,0:T(8,128)(2,1)S(1)}, u32[]{:S(2)}, u32[]{:S(2)}) %collective-permute-start.4) | collective-permute-done | bytes 417824 | tf_op jit(solution)/shard_map/xa1/ppermute | solution.py:50
  29.0 4.3 %collective-permute-start.5 = (bf16[272,768]{1,0:T(8,128)(2,1)S(1)}, bf16[272,768]{1,0:T(8,128)(2,1)S(1)}, u32[]{:S(2)}, u32[]{:S(2)}) collective-permute-start(bf16[272,768]{1,0:T(8,128)(2,1)S(1)} %collective-permute-done.4), channel_id=1, source_target_pairs={{0,9},{1,8},{2,11},{3,10},{4,13},{5,12},{6,15},{7,14},{8,1},{9,0},... | collective-permute-start | bytes 1253384 | tf_op jit(solution)/shard_map/sigma1/ppermute | solution.py:50
  33.3 1.0 %copy-done = bf16[272,768]{1,0:T(8,128)(2,1)S(1)} copy-done((bf16[272,768]{1,0:T(8,128)(2,1)S(1)}, bf16[272,768]{1,0:T(8,128)(2,1)}, u32[]{:S(2)}) %copy-start) | copy-done | bytes 417816
  34.3 0.1 relay.6
  34.4 0.7 collective-permute-start.11
  35.1 0.6 collective-permute-start.13
  35.8 0.0 collective-permute-done.9.b.b3
  35.8 1.3 %collective-permute-start.10 = (bf16[256,768]{1,0:T(8,128)(2,1)S(1)}, bf16[256,768]{1,0:T(8,128)(2,1)S(1)}, u32[]{:S(2)}, u32[]{:S(2)}) collective-permute-start(bf16[256,768]{1,0:T(8,128)(2,1)S(1)} %get-tuple-element.40), channel_id=1, source_target_pairs={{0,16},{1,241},{2,18},{3,243},{4,20},{5,245},{6,22},{7,247},{8,24}... | collective-permute-start | bytes 1179656 | tf_op jit(solution)/shard_map/xk0/ppermute | solution.py:50
  37.0 4.4 %collective-permute-done.5.a.a1 = bf16[272,768]{1,0:T(8,128)(2,1)S(1)} collective-permute-done((bf16[272,768]{1,0:T(8,128)(2,1)S(1)}, bf16[272,768]{1,0:T(8,128)(2,1)S(1)}, u32[]{:S(2)}, u32[]{:S(2)}) %collective-permute-start.5) | collective-permute-done | bytes 417824 | tf_op jit(solution)/shard_map/sigma1/ppermute | solution.py:50
  41.5 3.4 %collective-permute-start.2 = (f32[1,3072]{1,0:T(1,128)S(1)}, f32[1,3072]{1,0:T(1,128)S(1)}, u32[]{:S(2)}, u32[]{:S(2)}) collective-permute-start(f32[1,3072]{1,0:T(1,128)S(1)} %copy-done.2), channel_id=1, source_target_pairs={{0,9},{1,8},{2,11},{3,10},{4,13},{5,12},{6,15},{7,14},{8,1},{9,0},... | collective-permute-start | bytes 36872 | tf_op jit(solution)/shard_map/gain/ppermute | solution.py:50
  45.0 0.1 collective-permute-start.6
  45.1 1.5 %collective-permute-start.12 = (bf16[272,768]{1,0:T(8,128)(2,1)S(1)}, bf16[272,768]{1,0:T(8,128)(2,1)S(1)}, u32[]{:S(2)}, u32[]{:S(2)}) collective-permute-start(bf16[272,768]{1,0:T(8,128)(2,1)S(1)} %forward.2), channel_id=1, source_target_pairs={{0,16},{1,241},{2,18},{3,243},{4,20},{5,245},{6,22},{7,247},{8,24}... | collective-permute-start | bytes 1253384 | tf_op jit(solution)/shard_map/xt0/ppermute | solution.py:50
  46.6 3.8 %collective-permute-done.13.a.a3 = bf16[272,768]{1,0:T(8,128)(2,1)S(1)} collective-permute-done((bf16[272,768]{1,0:T(8,128)(2,1)S(1)}, bf16[272,768]{1,0:T(8,128)(2,1)S(1)}, u32[]{:S(2)}, u32[]{:S(2)}) %collective-permute-start.13) | collective-permute-done | bytes 417824 | tf_op jit(solution)/shard_map/sigma3/ppermute | solution.py:50
  50.4 1.8 %collective-permute-start.16 = (bf16[272,768]{1,0:T(8,128)(2,1)S(1)}, bf16[272,768]{1,0:T(8,128)(2,1)S(1)}, u32[]{:S(2)}, u32[]{:S(2)}) collective-permute-start(bf16[272,768]{1,0:T(8,128)(2,1)S(1)} %forward.3), channel_id=1, source_target_pairs={{0,20},{1,245},{2,22},{3,247},{4,16},{5,241},{6,18},{7,243},{8,28}... | collective-permute-start | bytes 1253384 | tf_op jit(solution)/shard_map/xt2/ppermute | solution.py:50
  52.2 0.1 relay.7
  52.3 0.3 collective-permute-start.14
  52.5 0.2 collective-permute-done.6.t1
  52.8 2.2 %early.1.acc = f32[768,768]{1,0:T(8,128)S(1)} custom-call(f32[1,3072]{1,0:T(1,128)S(1)} %copy-done.2, f32[1,3072]{1,0:T(1,128)S(1)} %collective-permute-done.2.other, bf16[272,768]{1,0:T(8,128)(2,1)S(1)} %collective-permute-done.3.b.b1, bf16[272,768]{1,0:T(8,128)(2,1)S(1)} %collective-permute-done.5.a.a1, bf16[272,768]{1,0:T(8,128)(2,1)S(1)} %collective-permute-done.6.t1, ...), custom_call_target="tpu_custom_call" | custom-call | tf_op jit(solution)/shard_map/early/pallas_call | solution.py:297
  55.0 9.9 %collective-permute-done.16.t2 = bf16[272,768]{1,0:T(8,128)(2,1)S(1)} collective-permute-done((bf16[272,768]{1,0:T(8,128)(2,1)S(1)}, bf16[272,768]{1,0:T(8,128)(2,1)S(1)}, u32[]{:S(2)}, u32[]{:S(2)}) %collective-permute-start.16) | collective-permute-done | bytes 417824 | tf_op jit(solution)/shard_map/xt2/ppermute | solution.py:50
  64.9 12.7 %last.1 = f32[768,768]{1,0:T(8,128)} custom-call(f32[768,768]{1,0:T(8,128)S(1)} %early.1.acc, f32[1,3072]{1,0:T(1,128)S(1)} %copy-done.2, f32[1,3072]{1,0:T(1,128)S(1)} %collective-permute-done.2.other, bf16[272,768]{1,0:T(8,128)(2,1)S(1)} %collective-permute-done.9.b.b3, bf16[272,768]{1,0:T(8,128)(2,1)S(1)} %collective-permute-done.13.a.a3, ...), custom_call_target="tpu_custom_call" | custom-call | tf_op jit(solution)/shard_map/last/pallas_call | solution.py:297
  (17 shorter events, 0.1 us)
Async XLA Ops:
  3.7 37.7 %copy-start.2 = (f32[1,3072]{1,0:T(1,128)S(1)}, f32[1,3072]{1,0:T(1,128)}, u32[]{:S(2)}) copy-start(f32[1,3072]{1,0:T(1,128)} %gain.3) | copy-start | bytes 36868
  3.8 13.7 %collective-permute-start.8 = (bf16[272,768]{1,0:T(8,128)(2,1)}, bf16[272,768]{1,0:T(8,128)(2,1)S(1)}, u32[]{:S(2)}, u32[]{:S(2)}) collective-permute-start(bf16[272,768]{1,0:T(8,128)(2,1)} %get-tuple-element.38), channel_id=1, source_target_pairs={{0,246},{1,23},{2,240},{3,17},{4,242},{5,19},{6,244},{7,21},{8,254... | collective-permute-start | bytes 1253384 | tf_op jit(solution)/shard_map/xa3/ppermute | solution.py:50
  7.7 14.7 %collective-permute-start = (bf16[272,768]{1,0:T(8,128)(2,1)}, bf16[272,768]{1,0:T(8,128)(2,1)S(1)}, u32[]{:S(2)}, u32[]{:S(2)}) collective-permute-start(bf16[272,768]{1,0:T(8,128)(2,1)} %get-tuple-element.26), channel_id=1, source_target_pairs={{0,9},{1,8},{2,11},{3,10},{4,13},{5,12},{6,15},{7,14},{8,1},{9,0},... | collective-permute-start | bytes 1253384 | tf_op jit(solution)/shard_map/sigma2/ppermute | solution.py:50
  11.8 17.2 %collective-permute-start.4 = (bf16[272,768]{1,0:T(8,128)(2,1)}, bf16[272,768]{1,0:T(8,128)(2,1)S(1)}, u32[]{:S(2)}, u32[]{:S(2)}) collective-permute-start(bf16[272,768]{1,0:T(8,128)(2,1)} %get-tuple-element.31), channel_id=1, source_target_pairs={{0,242},{1,19},{2,244},{3,21},{4,246},{5,23},{6,240},{7,17},{8,250... | collective-permute-start | bytes 1253384 | tf_op jit(solution)/shard_map/xa1/ppermute | solution.py:50
  11.8 21.5 %collective-permute-start.7 = (bf16[272,768]{1,0:T(8,128)(2,1)}, bf16[272,768]{1,0:T(8,128)(2,1)S(1)}, u32[]{:S(2)}, u32[]{:S(2)}) collective-permute-start(bf16[272,768]{1,0:T(8,128)(2,1)} %get-tuple-element.34), channel_id=1, source_target_pairs={{0,9},{1,8},{2,11},{3,10},{4,13},{5,12},{6,15},{7,14},{8,1},{9,0},... | collective-permute-start | bytes 1253384 | tf_op jit(solution)/shard_map/sigma0/ppermute | solution.py:50
  11.8 23.3 %collective-permute-start.3 = (bf16[272,768]{1,0:T(8,128)(2,1)}, bf16[272,768]{1,0:T(8,128)(2,1)S(1)}, u32[]{:S(2)}, u32[]{:S(2)}) collective-permute-start(bf16[272,768]{1,0:T(8,128)(2,1)} %get-tuple-element.30), channel_id=1, source_target_pairs={{0,18},{1,243},{2,20},{3,245},{4,22},{5,247},{6,16},{7,241},{8,26}... | collective-permute-start | bytes 1253384 | tf_op jit(solution)/shard_map/xb1/ppermute | solution.py:50
  17.5 18.3 %collective-permute-start.9 = (bf16[272,768]{1,0:T(8,128)(2,1)}, bf16[272,768]{1,0:T(8,128)(2,1)S(1)}, u32[]{:S(2)}, u32[]{:S(2)}) collective-permute-start(bf16[272,768]{1,0:T(8,128)(2,1)} %get-tuple-element.39), channel_id=1, source_target_pairs={{0,22},{1,247},{2,16},{3,241},{4,18},{5,243},{6,20},{7,245},{8,30}... | collective-permute-start | bytes 1253384 | tf_op jit(solution)/shard_map/xb3/ppermute | solution.py:50
  22.4 1.0 %copy-start.1 = (bf16[272,768]{1,0:T(8,128)(2,1)S(1)}, bf16[272,768]{1,0:T(8,128)(2,1)}, u32[]{:S(2)}) copy-start(bf16[272,768]{1,0:T(8,128)(2,1)} %get-tuple-element.27.b) | copy-start | bytes 1253380
  23.5 12.2 %collective-permute-start.1 = (bf16[272,768]{1,0:T(8,128)(2,1)S(1)}, bf16[272,768]{1,0:T(8,128)(2,1)S(1)}, u32[]{:S(2)}, u32[]{:S(2)}) collective-permute-start(bf16[272,768]{1,0:T(8,128)(2,1)S(1)} %get-tuple-element.28.own), channel_id=1, source_target_pairs={{0,8},{1,9},{2,10},{3,11},{4,12},{5,13},{6,14},{7,15},{8,0},{9,1},... | collective-permute-start | bytes 1253384 | tf_op jit(solution)/shard_map/tau2/ppermute | solution.py:50
  29.0 12.4 %collective-permute-start.5 = (bf16[272,768]{1,0:T(8,128)(2,1)S(1)}, bf16[272,768]{1,0:T(8,128)(2,1)S(1)}, u32[]{:S(2)}, u32[]{:S(2)}) collective-permute-start(bf16[272,768]{1,0:T(8,128)(2,1)S(1)} %collective-permute-done.4), channel_id=1, source_target_pairs={{0,9},{1,8},{2,11},{3,10},{4,13},{5,12},{6,15},{7,14},{8,1},{9,0},... | collective-permute-start | bytes 1253384 | tf_op jit(solution)/shard_map/sigma1/ppermute | solution.py:50
  33.3 1.0 %copy-start = (bf16[272,768]{1,0:T(8,128)(2,1)S(1)}, bf16[272,768]{1,0:T(8,128)(2,1)}, u32[]{:S(2)}) copy-start(bf16[272,768]{1,0:T(8,128)(2,1)} %get-tuple-element.35.b) | copy-start | bytes 1253380
  34.4 10.5 %collective-permute-start.11 = (bf16[272,768]{1,0:T(8,128)(2,1)S(1)}, bf16[272,768]{1,0:T(8,128)(2,1)S(1)}, u32[]{:S(2)}, u32[]{:S(2)}) collective-permute-start(bf16[272,768]{1,0:T(8,128)(2,1)S(1)} %get-tuple-element.41.own), channel_id=1, source_target_pairs={{0,8},{1,9},{2,10},{3,11},{4,12},{5,13},{6,14},{7,15},{8,0},{9,1},... | collective-permute-start | bytes 1253384 | tf_op jit(solution)/shard_map/tau0/ppermute | solution.py:50
  35.1 15.3 %collective-permute-start.13 = (bf16[272,768]{1,0:T(8,128)(2,1)S(1)}, bf16[272,768]{1,0:T(8,128)(2,1)S(1)}, u32[]{:S(2)}, u32[]{:S(2)}) collective-permute-start(bf16[272,768]{1,0:T(8,128)(2,1)S(1)} %collective-permute-done.8), channel_id=1, source_target_pairs={{0,9},{1,8},{2,11},{3,10},{4,13},{5,12},{6,15},{7,14},{8,1},{9,0},... | collective-permute-start | bytes 1253384 | tf_op jit(solution)/shard_map/sigma3/ppermute | solution.py:50
  35.8 9.4 %collective-permute-start.15 = (bf16[256,768]{1,0:T(8,128)(2,1)S(1)}, bf16[256,768]{1,0:T(8,128)(2,1)S(1)}, u32[]{:S(2)}, u32[]{:S(2)}) collective-permute-start(bf16[256,768]{1,0:T(8,128)(2,1)S(1)} %get-tuple-element.45), channel_id=1, source_target_pairs={{0,20},{1,245},{2,22},{3,247},{4,16},{5,241},{6,18},{7,243},{8,28}... | collective-permute-start | bytes 1179656 | tf_op jit(solution)/shard_map/xk2/ppermute | solution.py:50
  35.8 16.5 %collective-permute-start.10 = (bf16[256,768]{1,0:T(8,128)(2,1)S(1)}, bf16[256,768]{1,0:T(8,128)(2,1)S(1)}, u32[]{:S(2)}, u32[]{:S(2)}) collective-permute-start(bf16[256,768]{1,0:T(8,128)(2,1)S(1)} %get-tuple-element.40), channel_id=1, source_target_pairs={{0,16},{1,241},{2,18},{3,243},{4,20},{5,245},{6,22},{7,247},{8,24}... | collective-permute-start | bytes 1179656 | tf_op jit(solution)/shard_map/xk0/ppermute | solution.py:50
  41.5 10.8 %collective-permute-start.2 = (f32[1,3072]{1,0:T(1,128)S(1)}, f32[1,3072]{1,0:T(1,128)S(1)}, u32[]{:S(2)}, u32[]{:S(2)}) collective-permute-start(f32[1,3072]{1,0:T(1,128)S(1)} %copy-done.2), channel_id=1, source_target_pairs={{0,9},{1,8},{2,11},{3,10},{4,13},{5,12},{6,15},{7,14},{8,1},{9,0},... | collective-permute-start | bytes 36872 | tf_op jit(solution)/shard_map/gain/ppermute | solution.py:50
  45.0 7.8 %collective-permute-start.6 = (bf16[272,768]{1,0:T(8,128)(2,1)S(1)}, bf16[272,768]{1,0:T(8,128)(2,1)S(1)}, u32[]{:S(2)}, u32[]{:S(2)}) collective-permute-start(bf16[272,768]{1,0:T(8,128)(2,1)S(1)} %relay.5), channel_id=1, source_target_pairs={{0,8},{1,9},{2,10},{3,11},{4,12},{5,13},{6,14},{7,15},{8,0},{9,1},... | collective-permute-start | bytes 1253384 | tf_op jit(solution)/shard_map/tau1/ppermute | solution.py:50
  45.1 7.7 %collective-permute-start.12 = (bf16[272,768]{1,0:T(8,128)(2,1)S(1)}, bf16[272,768]{1,0:T(8,128)(2,1)S(1)}, u32[]{:S(2)}, u32[]{:S(2)}) collective-permute-start(bf16[272,768]{1,0:T(8,128)(2,1)S(1)} %forward.2), channel_id=1, source_target_pairs={{0,16},{1,241},{2,18},{3,243},{4,20},{5,245},{6,22},{7,247},{8,24}... | collective-permute-start | bytes 1253384 | tf_op jit(solution)/shard_map/xt0/ppermute | solution.py:50
  50.4 14.5 %collective-permute-start.16 = (bf16[272,768]{1,0:T(8,128)(2,1)S(1)}, bf16[272,768]{1,0:T(8,128)(2,1)S(1)}, u32[]{:S(2)}, u32[]{:S(2)}) collective-permute-start(bf16[272,768]{1,0:T(8,128)(2,1)S(1)} %forward.3), channel_id=1, source_target_pairs={{0,20},{1,245},{2,22},{3,247},{4,16},{5,241},{6,18},{7,243},{8,28}... | collective-permute-start | bytes 1253384 | tf_op jit(solution)/shard_map/xt2/ppermute | solution.py:50
  52.3 12.6 %collective-permute-start.14 = (bf16[272,768]{1,0:T(8,128)(2,1)S(1)}, bf16[272,768]{1,0:T(8,128)(2,1)S(1)}, u32[]{:S(2)}, u32[]{:S(2)}) collective-permute-start(bf16[272,768]{1,0:T(8,128)(2,1)S(1)} %relay.7), channel_id=1, source_target_pairs={{0,8},{1,9},{2,10},{3,11},{4,12},{5,13},{6,14},{7,15},{8,0},{9,1},... | collective-permute-start | bytes 1253384 | tf_op jit(solution)/shard_map/tau3/ppermute | solution.py:50

commit v4 on v3

v4 whole, which is shorter than its diff:
```python
import functools

import jax
import jax.numpy as jnp
from jax import lax
from jax.experimental import pallas as pl
from jax.experimental.pallas import tpu as pltpu
from jax.sharding import PartitionSpec as P

D = 6144
BLK = 768
TOKENS = 2048
SECTIONS, REPLICAS, HALVES = 16, 8, 2
ROWS = TOKENS // REPLICAS
COLS = D // HALVES
EXTRA = 16
AXES = ("section", "dp", "tensor")
BESIDE = pl.CostEstimate(flops=2 * 10**10, transcendentals=0, bytes_accessed=2**20)


def pairs(move):
    out = []
    for s in range(SECTIONS):
        for d in range(REPLICAS):
            for h in range(HALVES):
                to_s, x, y = move(s, d % 4, 2 * h + d // 4)
                to = ((to_s % SECTIONS) * REPLICAS + (y % 2) * 4 + x % 4) * HALVES + y // 2
                out.append(((s * REPLICAS + d) * HALVES + h, to))
    return out


def across(shift, own):
    def move(s, x, y):
        kind = y // 2 if own else 1 - y // 2
        return (s + 1 if kind == 0 else s - 1), x + shift, y

    return pairs(move)


SIGMA = pairs(lambda s, x, y: (s, x, y ^ 3))
TAU = pairs(lambda s, x, y: (s, x, y ^ 1))


FIRST_CUTS = [(False, 2), (False, 1), (False, 3)]
SECOND_CUTS = [(False, 0), (True, 1), (True, 3), (True, 0), (True, 2)]


def send(name, block, route, *after):
    with jax.named_scope(name):
        if after:
            block = lax.optimization_barrier((block, *after))[0]
        return lax.ppermute(block, AXES, route)


def split_three(values):
    parts = []
    for _ in range(3):
        parts.append(values.astype(jnp.bfloat16))
        values = values - parts[-1].astype(jnp.float32)
    return parts


def coded(rows):
    return jnp.concatenate(split_three(rows), axis=1)


def decoded(block):
    block = block.astype(jnp.float32)
    return block[:, :ROWS] + block[:, ROWS : 2 * ROWS] + block[:, 2 * ROWS :]


PARTS = 4


def cut_chunks(cuts, sources, held, sems):
    emb, outs, grads, loss = sources
    s = lax.axis_index("section")
    x = lax.rem(lax.axis_index("dp"), 4)
    h = lax.axis_index("tensor")

    def load(r, source):
        cols = pl.ds(pl.multiple_of(lax.rem(x + cuts[r][1], 4) * BLK, BLK), BLK)
        return pltpu.make_async_copy(source.at[:, cols], held.at[r], sems.at[r])

    for r, (own, _) in enumerate(cuts):
        kind = h if own else 1 - h
        edge = jnp.where(kind == 0, s == SECTIONS - 1, s == 0)
        for k, e, source in ((0, True, emb), (0, False, outs), (1, True, loss), (1, False, grads)):
            @pl.when((kind == k) & (edge == e))
            def _():
                load(r, source).start()
    return lambda r: load(r, outs).wait()


def first_cut_kernel(*refs):
    sources, chunks, tail_out = refs[:4], refs[4:7], refs[7]
    held, hidden, tail, in_sems, hidden_sems, out_sems, tail_sems = refs[8:]
    step = ROWS // PARTS

    def load(source, part):
        rows = pl.ds(part * step, step)
        return pltpu.make_async_copy(source.at[rows], hidden.at[rows], hidden_sems.at[part])

    wait = cut_chunks(FIRST_CUTS, sources, held, in_sems)
    last = lax.axis_index("section") == SECTIONS - 1
    for edge, source in ((True, sources[0]), (False, sources[1])):
        @pl.when(last == edge)
        def _():
            for part in range(PARTS):
                load(source, part).start()
    stores = []
    for r, chunk in enumerate(chunks):
        wait(r)
        stores.append(pltpu.make_async_copy(held.at[r], chunk.at[:ROWS], out_sems.at[r]))
        stores[-1].start()
    sums = []
    for part in range(PARTS):
        load(sources[1], part).wait()
        values = hidden[part * step : (part + 1) * step, :].astype(jnp.float32)
        total = jnp.sum(values, axis=1, keepdims=True)
        power = jnp.sum(values * values, axis=1, keepdims=True)
        odd = lax.broadcasted_iota(jnp.int32, (step, 128), 1) % 2 == 1
        sums.append(jnp.where(odd, power, total))
    tail[...] = coded(jnp.concatenate(sums, axis=0).T[:EXTRA, :])
    for i, target in enumerate((chunks[1].at[ROWS:], chunks[2].at[ROWS:], tail_out)):
        stores.append(pltpu.make_async_copy(tail, target, tail_sems.at[i]))
        stores[-1].start()
    for copy in stores:
        copy.wait()


def second_cut_kernel(*refs):
    sources, tail, chunks = refs[:4], refs[4], refs[5:10]
    held, in_sems, out_sems, tail_sems = refs[10:]
    wait = cut_chunks(SECOND_CUTS, sources, held, in_sems)
    stores = []
    for r, chunk in enumerate(chunks[:-1]):
        stores.append(pltpu.make_async_copy(tail, chunk.at[ROWS:], tail_sems.at[r]))
        stores[-1].start()
    for r, chunk in enumerate(chunks):
        wait(r)
        stores.append(pltpu.make_async_copy(held.at[r], chunk.at[:ROWS], out_sems.at[r]))
        stores[-1].start()
    for copy in stores:
        copy.wait()


def cut(*sources):
    any_spec = pl.BlockSpec(memory_space=pl.ANY)
    plain = jax.ShapeDtypeStruct((ROWS, BLK), jnp.bfloat16)
    summed = jax.ShapeDtypeStruct((ROWS + EXTRA, BLK), jnp.bfloat16)
    tail = jax.ShapeDtypeStruct((EXTRA, BLK), jnp.bfloat16)
    dma = pltpu.SemaphoreType.DMA
    *first, sums = pl.pallas_call(
        first_cut_kernel,
        out_shape=[plain, summed, summed, tail],
        in_specs=[any_spec] * 4,
        out_specs=[any_spec] * 4,
        scratch_shapes=[
            pltpu.VMEM((3, ROWS, BLK), jnp.bfloat16),
            pltpu.VMEM((ROWS, COLS), jnp.bfloat16),
            pltpu.VMEM((EXTRA, BLK), jnp.bfloat16),
            *(dma((n,)) for n in (3, PARTS, 3, 3)),
        ],
        name="cut1",
    )(*sources)
    second = pl.pallas_call(
        second_cut_kernel,
        out_shape=[summed] * 4 + [plain],
        in_specs=[any_spec] * 4 + [pl.BlockSpec(memory_space=pltpu.VMEM)],
        out_specs=[any_spec] * 5,
        scratch_shapes=[
            pltpu.VMEM((5, ROWS, BLK), jnp.bfloat16),
            *(dma((n,)) for n in (5, 5, 4)),
        ],
        name="cut2",
    )(*sources, sums)
    return *first, *second


def relay_kernel(a, b, onward, *kept):
    keeper = keeps()
    onward[:ROWS, :] = jnp.where(keeper, a[:ROWS, :], b[:ROWS, :])
    if onward.shape[0] > ROWS:
        crossed = lax.broadcasted_iota(jnp.int32, (EXTRA, BLK), 0) % 4 >= 2
        onward[ROWS:, :] = jnp.where(crossed, a[ROWS:, :], b[ROWS:, :])
    for out in kept:
        out[...] = jnp.where(keeper, b[...], a[...])


def relay(a, b, with_kept=False):
    vmem = pl.BlockSpec(memory_space=pltpu.VMEM)
    shapes = [jax.ShapeDtypeStruct(a.shape, a.dtype)] * (1 + with_kept)
    return pl.pallas_call(
        relay_kernel,
        out_shape=shapes,
        in_specs=[vmem] * 2,
        out_specs=[vmem] * len(shapes),
        compiler_params=pltpu.CompilerParams(vmem_limit_bytes=4 * 2**20),
        cost_estimate=BESIDE,
        name="relay",
    )(a, b)


def bundle_kernel(a0, b0, t0, own, t2, out0, out2):
    first = lax.broadcasted_iota(jnp.int32, (EXTRA, BLK), 0) < 4
    sums = jnp.where(first, t0[ROWS:, :], own[ROWS:, :])
    out2[:ROWS, :] = t2[...]
    out2[ROWS:, :] = sums
    out0[:ROWS, :] = jnp.where(keeps(), b0[:ROWS, :], a0[:ROWS, :])
    out0[ROWS : 2 * ROWS, :] = t0[:ROWS, :]
    out0[2 * ROWS :, :] = sums


def bundle(a0, b0, t0, own, t2):
    vmem = pl.BlockSpec(memory_space=pltpu.VMEM)
    return pl.pallas_call(
        bundle_kernel,
        out_shape=[
            jax.ShapeDtypeStruct((rows + EXTRA, BLK), jnp.bfloat16) for rows in (2 * ROWS, ROWS)
        ],
        in_specs=[vmem] * 5,
        out_specs=[vmem] * 2,
        compiler_params=pltpu.CompilerParams(vmem_limit_bytes=6 * 2**20),
        cost_estimate=BESIDE,
        name="bundle",
    )(a0, b0, t0, own, t2)


GAIN_ROW = 8


def own_gain(gain):
    x = lax.rem(lax.axis_index("dp"), 4)
    return gain[:, pl.ds(pl.multiple_of(x * BLK, BLK), BLK)]


def mark_kernel(chunk, gain, out, tail, sems):
    del chunk
    load = pltpu.make_async_copy(out.at[ROWS:], tail, sems.at[0])
    load.start()
    load.wait()
    row = lax.broadcasted_iota(jnp.int32, (EXTRA, BLK), 0)
    values = tail[...].astype(jnp.float32)
    for i, part in enumerate(split_three(own_gain(gain))):
        values = jnp.where(row == GAIN_ROW + i, part.astype(jnp.float32), values)
    tail[...] = values.astype(jnp.bfloat16)
    store = pltpu.make_async_copy(tail, out.at[ROWS:], sems.at[1])
    store.start()
    store.wait()


def mark(chunk, gain):
    any_spec = pl.BlockSpec(memory_space=pl.ANY)
    return pl.pallas_call(
        mark_kernel,
        out_shape=jax.ShapeDtypeStruct(chunk.shape, chunk.dtype),
        in_specs=[any_spec, pl.BlockSpec(memory_space=pltpu.VMEM)],
        out_specs=any_spec,
        scratch_shapes=[
            pltpu.VMEM((EXTRA, BLK), jnp.bfloat16),
            pltpu.SemaphoreType.DMA((2,)),
        ],
        input_output_aliases={0: 0},
        compiler_params=pltpu.CompilerParams(vmem_limit_bytes=4 * 2**20),
        cost_estimate=BESIDE,
        name="mark",
    )(chunk, gain)


def gain_columns(gain, marked):
    parts = marked[ROWS:, :].astype(jnp.float32)[GAIN_ROW : GAIN_ROW + 3]
    crossed = parts[0:1] + parts[1:2] + parts[2:3]
    return jnp.where(lax.div(lax.axis_index("dp"), 4) == 0, own_gain(gain), crossed)


def pair_rows(first, second, mine, crossed, beside, relayed, gain_row):
    is_input = lax.axis_index("tensor") == 0
    same, swapped = mine + relayed, crossed + beside
    stats = jnp.concatenate(
        [jnp.where(keeps(), same, swapped), jnp.where(keeps(), swapped, same)] * 2, axis=0
    ).T / D
    gain = jnp.where(is_input, gain_row, 1.0)
    rows = []
    for chunk, c in ((first, 0), (second, 2)):
        mean, power = stats[:, c : c + 1], stats[:, c + 1 : c + 2]
        scale = jnp.where(is_input, lax.rsqrt(power - mean * mean + 1e-05), 1.0)
        mean = jnp.where(is_input, mean, 0.0)
        rows.append(((chunk.astype(jnp.float32) - mean) * scale * gain).astype(jnp.bfloat16))
    return rows


def gram(rows):
    rows = jnp.concatenate(rows, axis=0)
    return lax.dot_general(
        rows, rows, (((0,), (0,)), ((), ())), preferred_element_type=jnp.float32
    )


def keeps():
    return lax.axis_index("tensor") == lax.div(lax.axis_index("dp"), 4)


def early_rows(b, a, t, row):
    mine, crossed, rest = (decoded(r[ROWS:, :]) for r in (b, a, t))
    kept = jnp.where(keeps(), b[:ROWS, :], a[:ROWS, :])
    return pair_rows(kept, t[:ROWS, :], mine[:2], crossed[:2], rest[:2], rest[2:4], row)


def late_rows(k, t, row):
    rest = decoded(t[ROWS:, :])
    return pair_rows(k[...], t[:ROWS, :], rest[4:6], rest[6:8], rest[:2], rest[2:4], row)


def early_kernel(gain, b1, a1, t1, out):
    out[...] = gram(early_rows(b1, a1, t1, gain_columns(gain, a1)))


def middle_kernel(acc, gain, a1, k2, t2, out):
    out[...] = acc[...] + gram(late_rows(k2, t2, gain_columns(gain, a1)))


def split(a):
    hi = a.astype(jnp.bfloat16)
    return hi, (a - hi.astype(jnp.float32)).astype(jnp.bfloat16)


TILE = 256
STRIPES = [(slice(i, i + TILE), slice(0, i + TILE)) for i in range(0, BLK, TILE)]


def product(a, b, rows, cols):
    left = jnp.concatenate([a[0][rows, :], a[0][rows, :], a[1][rows, :]], axis=1)
    right = jnp.concatenate([b[0][:, cols], b[1][:, cols], b[0][:, cols]], axis=0)
    return jnp.dot(left, right, preferred_element_type=jnp.float32)


def put_symmetric(refs, rows, cols, value, parts):
    for ref, part in zip(refs, parts(value)):
        ref[rows, cols] = part
    if rows.start:
        before = slice(0, rows.start)
        for ref, part in zip(refs, parts(value[:, before].T)):
            ref[before, rows] = part


def invert(out, first, second, fourth, low_parts, low, whole, sems):
    row = lax.broadcasted_iota(jnp.int32, (BLK, BLK), 0)
    col = lax.broadcasted_iota(jnp.int32, (BLK, BLK), 1)
    eye = jnp.where(row == col, 1.0, 0.0).astype(jnp.float32)
    damped = whole[...] * (1.0 / TOKENS) + 0.05 * eye
    bound = jnp.max(jnp.sum(jnp.abs(damped), axis=0, keepdims=True))
    inverse_bound = 1.0 / bound
    error = eye - damped * inverse_bound
    first[0][...], first[1][...] = split(error)
    low[...] = eye + error
    for rows, cols in STRIPES:
        value = product(first, first, rows, cols)
        put_symmetric(second, rows, cols, value, split)
        low[rows, cols] += value
    for rows, cols in STRIPES:
        value = low[rows, cols] + product(first, second, rows, cols)
        low[rows, cols] = value
        put_symmetric(low_parts, rows, cols, value, split)
        put_symmetric(fourth, rows, cols, product(second, second, rows, cols), split)
    copies = []
    for rows, cols in reversed(STRIPES):
        value = (low[rows, cols] + product(low_parts, fourth, rows, cols)) * inverse_bound
        put_symmetric([whole], rows, cols, value, lambda block: [block])
        copies.append(pltpu.make_async_copy(whole.at[rows], out.at[rows], sems.at[len(copies)]))
        copies[-1].start()
    for copy in copies:
        copy.wait()


def last_kernel(acc, gain, a1, b3, a3, t3, both0, out, *scratch):
    row = gain_columns(gain, a1)
    both0 = both0.at[:ROWS], both0.at[ROWS:]
    whole = scratch[9]
    whole[...] = acc[...] + gram(late_rows(*both0, row))
    whole[...] += gram(early_rows(b3, a3, t3, row))
    pairs_of = [scratch[i : i + 2] for i in range(0, 8, 2)]
    invert(out, *pairs_of, *scratch[8:])


def in_vmem(kernel, name, args, out_space=pltpu.VMEM, scratch=()):
    vmem = pl.BlockSpec(memory_space=pltpu.VMEM)
    return pl.pallas_call(
        kernel,
        out_shape=jax.ShapeDtypeStruct((BLK, BLK), jnp.float32),
        in_specs=[vmem] * len(args),
        out_specs=pl.BlockSpec(memory_space=out_space),
        scratch_shapes=scratch,
        compiler_params=pltpu.CompilerParams(vmem_limit_bytes=26 * 2**20),
        cost_estimate=pl.CostEstimate(
            flops=3 * 10**10, transcendentals=0, bytes_accessed=64 * 2**20
        ),
        name=name,
    )(*args)


def per_device(embeddings, section_outputs, norm_gain, input_grads, loss_grads):
    a2, a1, a3, a0, b1, b3, b0, b2 = cut(
        embeddings, section_outputs[0], input_grads[0], loss_grads
    )
    ra2 = send("sigma2", a2, SIGMA)
    xa1 = send("xa1", a1, across(1, False))
    xa3 = send("xa3", a3, across(3, False))
    ra0 = send("sigma0", a0, SIGMA)

    t2, k2 = relay(ra2, b2, True)
    rt2 = send("tau2", t2, TAU)
    ra1 = send("sigma1", mark(xa1, norm_gain), SIGMA, t2)
    xb1 = send("xb1", b1, across(1, True), xa1, xa3, t2)
    xb3 = send("xb3", b3, across(3, True), xa3, t2)
    (t0,) = relay(*lax.optimization_barrier((ra0, b0, rt2))[:2])
    rt0 = send("tau0", t0, TAU)
    ra3 = send("sigma3", xa3, SIGMA, ra0)
    xk2 = send("xk2", k2, across(2, True), xb1, xb3)
    rt1 = send("tau1", *relay(*lax.optimization_barrier((ra1, xb1, xb3))[:2]), TAU)
    both0, rt2 = bundle(ra0, b0, rt0, t0, rt2)
    xt2 = send("xt2", rt2, across(2, True))
    rt3 = send("tau3", *relay(*lax.optimization_barrier((ra3, xb3, both0))[:2]), TAU)
    both0 = send("both0", both0, across(0, True))

    total = in_vmem(early_kernel, "early", (norm_gain, xb1, ra1, rt1))
    total = in_vmem(middle_kernel, "middle", (total, norm_gain, ra1, xk2, xt2))
    square = (BLK, BLK)
    result = in_vmem(
        last_kernel,
        "last",
        (total, norm_gain, ra1, xb3, ra3, rt3, both0),
        pl.ANY,
        [pltpu.VMEM(square, jnp.bfloat16)] * 8
        + [pltpu.VMEM(square, jnp.float32)] * 2
        + [pltpu.SemaphoreType.DMA((len(STRIPES),))],
    )
    return result.reshape(1, 1, 1, BLK, BLK)


def solution(mesh):
    placed = (
        P("dp", "tensor"),
        P("section", "dp", "tensor"),
        P("section", "tensor"),
        P("section", "dp", "tensor"),
        P("dp", "tensor"),
    )
    return jax.shard_map(
        per_device,
        mesh=mesh,
        in_specs=placed,
        out_specs=P("section", "tensor", "dp", None, None),
        check_vma=False,
    )
```

time: 78.4 us -> 75.7 us (0.966)
  starting transfers between devices: 30.4 us -> 19 us
  waiting for transfers between devices: 26.1 us -> 32.8 us
  Pallas kernels: 19 us -> 21.5 us
    ppermute x17 -> x15, starting transfers between devices: 30.4 us -> 19 us  [send(): return lax.ppermute(block, AXES, route)]
    ppermute x17 -> x15, waiting for transfers between devices: 26.1 us -> 32.8 us  [send(): return lax.ppermute(block, AXES, route)]
    pallas_call x3 -> x4, Pallas kernels: 3.8 us -> 6.63 us  [the longest x1 3.25 us: cut(): pl.pallas_call(first_cut_kernel, out_shape=[plain, summed, summed, tail],...]
    pallas_call x2 -> x3, Pallas kernels: 14.9 us -> 14.6 us  [in_vmem(): pl.pallas_call(kernel, out_shape=jax.ShapeDtypeStruct((BLK, BLK), jnp.flo...]
    unnamed x6 -> x10, local copies, waits for them, and re-layouts: 2.02 us -> 1.77 us
  transfers between devices with their start and end apart: 17 -> 15, of which waited for: 6 -> 9; matrix products, arithmetic and copies ran while one was open for 0% -> 0% of each run, Pallas kernels for 3% -> 8%
where the time goes in v4:
time: 75.7 us; the launch traced here: 75.4 us
  waiting for transfers between devices  32.8 us (43%)
  Pallas kernels  21.5 us (28%)
  starting transfers between devices  19 us (25%)
  local copies, waits for them, and re-layouts  1.77 us (2%)
    ppermute x15, waiting for transfers between devices, send(): return lax.ppermute(block, AXES, route)  32.8 us
    ppermute x15, starting transfers between devices, send(): return lax.ppermute(block, AXES, route)  19 us
    pallas_call x3, Pallas kernels, in_vmem(): pl.pallas_call(kernel, out_shape=jax.ShapeDtypeStruct((BLK, BLK), jnp.flo...  14.6 us
    pallas_call x1, Pallas kernels, cut(): pl.pallas_call(first_cut_kernel, out_shape=[plain, summed, summed, tail],...  3.25 us
    pallas_call x1, Pallas kernels, cut(): pl.pallas_call(second_cut_kernel, out_shape=[summed] * 4 + [plain], in_sp...  3.16 us
    unnamed x10, local copies, waits for them, and re-layouts  1.77 us
  transfers between devices with their start and end apart: 15, of which 9 were waited for; matrix products, arithmetic and copies ran while one was open for 0% of the time, Pallas kernels for 8%

profile of v4, /device:TPU:1, one launch (start us, length us, event | category | flops | bytes accessed | tf_op | source)
XLA Modules:
  0.0 75.4 jit_solution(16648068706974505658)
XLA Ops:
  0.0 3.2 %cut1.1 = (bf16[256,768]{1,0:T(8,128)(2,1)}, bf16[272,768]{1,0:T(8,128)(2,1)}, bf16[272,768]{1,0:T(8,128)(2,1)}, bf16[16,768]{1,0:T(8,128)(2,1)}) custom-call(bf16[256,3072]{1,0:T(8,128)(2,1)} %refs_0_.3, bf16[256,3072]{1,0:T(8,128)(2,1)} %bitcast.3, bf16[256,3072]{1,0:T(8,128)(2,1)} %bitcast.5, bf16[256,3072]{1,0:T(8,128)(2,1)} %refs_3_.3), custom_call_target="tpu_custom_call" | custom-call | tf_op jit(solution)/shard_map/cut1/pallas_call | solution.py:154
  3.3 3.3 %collective-permute-start.2 = (bf16[256,768]{1,0:T(8,128)(2,1)}, bf16[256,768]{1,0:T(8,128)(2,1)S(1)}, u32[]{:S(2)}, u32[]{:S(2)}) collective-permute-start(bf16[256,768]{1,0:T(8,128)(2,1)} %get-tuple-element.33), channel_id=1, source_target_pairs={{0,9},{1,8},{2,11},{3,10},{4,13},{5,12},{6,15},{7,14},{8,1},{9,0},... | collective-permute-start | bytes 1179656 | tf_op jit(solution)/shard_map/sigma2/ppermute | solution.py:52
  6.6 2.1 %collective-permute-start = (bf16[272,768]{1,0:T(8,128)(2,1)}, bf16[272,768]{1,0:T(8,128)(2,1)S(1)}, u32[]{:S(2)}, u32[]{:S(2)}) collective-permute-start(bf16[272,768]{1,0:T(8,128)(2,1)} %get-tuple-element.31), channel_id=1, source_target_pairs={{0,242},{1,19},{2,244},{3,21},{4,246},{5,23},{6,240},{7,17},{8,250... | collective-permute-start | bytes 1253384 | tf_op jit(solution)/shard_map/xa1/ppermute | solution.py:52
  8.6 6.8 %collective-permute-start.1 = (bf16[272,768]{1,0:T(8,128)(2,1)}, bf16[272,768]{1,0:T(8,128)(2,1)S(1)}, u32[]{:S(2)}, u32[]{:S(2)}) collective-permute-start(bf16[272,768]{1,0:T(8,128)(2,1)} %get-tuple-element.32), channel_id=1, source_target_pairs={{0,246},{1,23},{2,240},{3,17},{4,242},{5,19},{6,244},{7,21},{8,254... | collective-permute-start | bytes 1253384 | tf_op jit(solution)/shard_map/xa3/ppermute | solution.py:52
  15.4 3.2 %cut2.1 = (bf16[272,768]{1,0:T(8,128)(2,1)}, bf16[272,768]{1,0:T(8,128)(2,1)}, bf16[272,768]{1,0:T(8,128)(2,1)}, bf16[272,768]{1,0:T(8,128)(2,1)}, bf16[256,768]{1,0:T(8,128)(2,1)}) custom-call(bf16[256,3072]{1,0:T(8,128)(2,1)} %refs_0_.3, bf16[256,3072]{1,0:T(8,128)(2,1)} %bitcast.4, bf16[256,3072]{1,0:T(8,128)(2,1)} %bitcast.6, bf16[256,3072]{1,0:T(8,128)(2,1)} %refs_3_.3, ...), custom_call_target="tpu_custom_call" | custom-call | tf_op jit(solution)/shard_map/cut2/pallas_call | solution.py:167
  18.6 0.1 collective-permute-start.8
  18.7 1.0 %copy-done.1 = bf16[256,768]{1,0:T(8,128)(2,1)S(1)} copy-done((bf16[256,768]{1,0:T(8,128)(2,1)S(1)}, bf16[256,768]{1,0:T(8,128)(2,1)}, u32[]{:S(2)}) %copy-start.1) | copy-done | bytes 393240
  19.7 0.1 relay.4
  19.8 0.1 collective-permute-start.9
  19.9 3.6 %collective-permute-done.1 = bf16[272,768]{1,0:T(8,128)(2,1)S(1)} collective-permute-done((bf16[272,768]{1,0:T(8,128)(2,1)}, bf16[272,768]{1,0:T(8,128)(2,1)S(1)}, u32[]{:S(2)}, u32[]{:S(2)}) %collective-permute-start.1) | collective-permute-done | bytes 417824 | tf_op jit(solution)/shard_map/xa3/ppermute | solution.py:52
  23.6 0.1 mark.1
  23.7 0.1 collective-permute-start.4
  23.8 0.8 %copy-done.4 = bf16[272,768]{1,0:T(8,128)(2,1)S(1)} copy-done((bf16[272,768]{1,0:T(8,128)(2,1)S(1)}, bf16[272,768]{1,0:T(8,128)(2,1)}, u32[]{:S(2)}) %copy-start.4) | copy-done | bytes 417816
  24.5 0.8 collective-permute-start.3
  25.3 1.9 %collective-permute-start.5 = (bf16[272,768]{1,0:T(8,128)(2,1)S(1)}, bf16[272,768]{1,0:T(8,128)(2,1)S(1)}, u32[]{:S(2)}, u32[]{:S(2)}) collective-permute-start(bf16[272,768]{1,0:T(8,128)(2,1)S(1)} %copy-done.3), channel_id=1, source_target_pairs={{0,22},{1,247},{2,16},{3,241},{4,18},{5,243},{6,20},{7,245},{8,30}... | collective-permute-start | bytes 1253384 | tf_op jit(solution)/shard_map/xb3/ppermute | solution.py:52
  27.2 3.7 %collective-permute-done.8.a.a0 = bf16[272,768]{1,0:T(8,128)(2,1)S(1)} collective-permute-done((bf16[272,768]{1,0:T(8,128)(2,1)}, bf16[272,768]{1,0:T(8,128)(2,1)S(1)}, u32[]{:S(2)}, u32[]{:S(2)}) %collective-permute-start.8) | collective-permute-done | bytes 417824 | tf_op jit(solution)/shard_map/sigma0/ppermute | solution.py:52
  31.0 2.5 %collective-permute-start.12 = (bf16[272,768]{1,0:T(8,128)(2,1)S(1)}, bf16[272,768]{1,0:T(8,128)(2,1)S(1)}, u32[]{:S(2)}, u32[]{:S(2)}) collective-permute-start(bf16[272,768]{1,0:T(8,128)(2,1)S(1)} %collective-permute-done.1), channel_id=1, source_target_pairs={{0,9},{1,8},{2,11},{3,10},{4,13},{5,12},{6,15},{7,14},{8,1},{9,0},... | collective-permute-start | bytes 1253384 | tf_op jit(solution)/shard_map/sigma3/ppermute | solution.py:52
  33.5 0.1 collective-permute-start.10
  33.6 5.0 %collective-permute-done.3.b.b1 = bf16[272,768]{1,0:T(8,128)(2,1)S(1)} collective-permute-done((bf16[272,768]{1,0:T(8,128)(2,1)S(1)}, bf16[272,768]{1,0:T(8,128)(2,1)S(1)}, u32[]{:S(2)}, u32[]{:S(2)}) %collective-permute-start.3) | collective-permute-done | bytes 417824 | tf_op jit(solution)/shard_map/xb1/ppermute | solution.py:52
  38.6 1.3 %collective-permute-done.4.a.a1 = bf16[272,768]{1,0:T(8,128)(2,1)S(1)} collective-permute-done((bf16[272,768]{1,0:T(8,128)(2,1)S(1)}, bf16[272,768]{1,0:T(8,128)(2,1)S(1)}, u32[]{:S(2)}, u32[]{:S(2)}) %collective-permute-start.4) | collective-permute-done | bytes 417824 | tf_op jit(solution)/shard_map/sigma1/ppermute | solution.py:52
  40.0 0.8 %collective-permute-start.6 = (bf16[272,768]{1,0:T(8,128)(2,1)S(1)}, bf16[272,768]{1,0:T(8,128)(2,1)S(1)}, u32[]{:S(2)}, u32[]{:S(2)}) collective-permute-start(bf16[272,768]{1,0:T(8,128)(2,1)S(1)} %relay.5), channel_id=1, source_target_pairs={{0,8},{1,9},{2,10},{3,11},{4,12},{5,13},{6,14},{7,15},{8,0},{9,1},... | collective-permute-start | bytes 1253384 | tf_op jit(solution)/shard_map/tau1/ppermute | solution.py:52
  40.8 4.4 %collective-permute-done.10.t0 = bf16[272,768]{1,0:T(8,128)(2,1)S(1)} collective-permute-done((bf16[272,768]{1,0:T(8,128)(2,1)S(1)}, bf16[272,768]{1,0:T(8,128)(2,1)S(1)}, u32[]{:S(2)}, u32[]{:S(2)}) %collective-permute-start.10) | collective-permute-done | bytes 417824 | tf_op jit(solution)/shard_map/tau0/ppermute | solution.py:52
  45.2 0.1 bundle.1
  45.3 0.1 collective-permute-start.11
  45.5 3.4 %collective-permute-done.12.a.a3 = bf16[272,768]{1,0:T(8,128)(2,1)S(1)} collective-permute-done((bf16[272,768]{1,0:T(8,128)(2,1)S(1)}, bf16[272,768]{1,0:T(8,128)(2,1)S(1)}, u32[]{:S(2)}, u32[]{:S(2)}) %collective-permute-start.12) | collective-permute-done | bytes 417824 | tf_op jit(solution)/shard_map/sigma3/ppermute | solution.py:52
  48.9 0.3 collective-permute-start.13
  49.2 4.9 %collective-permute-done.6.t1 = bf16[272,768]{1,0:T(8,128)(2,1)S(1)} collective-permute-done((bf16[272,768]{1,0:T(8,128)(2,1)S(1)}, bf16[272,768]{1,0:T(8,128)(2,1)S(1)}, u32[]{:S(2)}, u32[]{:S(2)}) %collective-permute-start.6) | collective-permute-done | bytes 417824 | tf_op jit(solution)/shard_map/tau1/ppermute | solution.py:52
  54.1 1.3 %early.1.acc = f32[768,768]{1,0:T(8,128)S(1)} custom-call(f32[1,3072]{1,0:T(1,128)S(1)} %copy-done.2, bf16[272,768]{1,0:T(8,128)(2,1)S(1)} %collective-permute-done.3.b.b1, bf16[272,768]{1,0:T(8,128)(2,1)S(1)} %collective-permute-done.4.a.a1, bf16[272,768]{1,0:T(8,128)(2,1)S(1)} %collective-permute-done.6.t1), custom_call_target="tpu_custom_call" | custom-call | flops 30000001024 | bytes 67108864 | tf_op jit(solution)/shard_map/early/pallas_call | solution.py:388
  55.4 2.0 %collective-permute-done.7.k2 = bf16[256,768]{1,0:T(8,128)(2,1)S(1)} collective-permute-done((bf16[256,768]{1,0:T(8,128)(2,1)S(1)}, bf16[256,768]{1,0:T(8,128)(2,1)S(1)}, u32[]{:S(2)}, u32[]{:S(2)}) %collective-permute-start.7) | collective-permute-done | bytes 393248 | tf_op jit(solution)/shard_map/xk2/ppermute | solution.py:52
  57.5 4.5 %collective-permute-done.11.t2 = bf16[272,768]{1,0:T(8,128)(2,1)S(1)} collective-permute-done((bf16[272,768]{1,0:T(8,128)(2,1)S(1)}, bf16[272,768]{1,0:T(8,128)(2,1)S(1)}, u32[]{:S(2)}, u32[]{:S(2)}) %collective-permute-start.11) | collective-permute-done | bytes 417824 | tf_op jit(solution)/shard_map/xt2/ppermute | solution.py:52
  61.9 1.3 %middle.1.acc = f32[768,768]{1,0:T(8,128)S(1)} custom-call(f32[768,768]{1,0:T(8,128)S(1)} %early.1.acc, f32[1,3072]{1,0:T(1,128)S(1)} %copy-done.2, bf16[272,768]{1,0:T(8,128)(2,1)S(1)} %collective-permute-done.4.a.a1, bf16[256,768]{1,0:T(8,128)(2,1)S(1)} %collective-permute-done.7.k2, bf16[272,768]{1,0:T(8,128)(2,1)S(1)} %collective-permute-done.11.t2), custom_call_target="tpu_custom_call" | custom-call | flops 30000001024 | bytes 67108864 | tf_op jit(solution)/shard_map/middle/pallas_call | solution.py:388
  63.3 11.9 %last.1 = f32[768,768]{1,0:T(8,128)} custom-call(f32[768,768]{1,0:T(8,128)S(1)} %middle.1.acc, f32[1,3072]{1,0:T(1,128)S(1)} %copy-done.2, bf16[272,768]{1,0:T(8,128)(2,1)S(1)} %collective-permute-done.4.a.a1, bf16[272,768]{1,0:T(8,128)(2,1)S(1)} %collective-permute-done.5.b.b3, bf16[272,768]{1,0:T(8,128)(2,1)S(1)} %collective-permute-done.12.a.a3, ...), custom_call_target="tpu_custom_call" | custom-call | flops 30000001024 | bytes 67108864 | tf_op jit(solution)/shard_map/last/pallas_call | solution.py:388
  (19 shorter events, 0.3 us)
Async XLA Ops:
  3.3 15.4 %collective-permute-start.2 = (bf16[256,768]{1,0:T(8,128)(2,1)}, bf16[256,768]{1,0:T(8,128)(2,1)S(1)}, u32[]{:S(2)}, u32[]{:S(2)}) collective-permute-start(bf16[256,768]{1,0:T(8,128)(2,1)} %get-tuple-element.33), channel_id=1, source_target_pairs={{0,9},{1,8},{2,11},{3,10},{4,13},{5,12},{6,15},{7,14},{8,1},{9,0},... | collective-permute-start | bytes 1179656 | tf_op jit(solution)/shard_map/sigma2/ppermute | solution.py:52
  6.6 13.3 %collective-permute-start = (bf16[272,768]{1,0:T(8,128)(2,1)}, bf16[272,768]{1,0:T(8,128)(2,1)S(1)}, u32[]{:S(2)}, u32[]{:S(2)}) collective-permute-start(bf16[272,768]{1,0:T(8,128)(2,1)} %get-tuple-element.31), channel_id=1, source_target_pairs={{0,242},{1,19},{2,244},{3,21},{4,246},{5,23},{6,240},{7,17},{8,250... | collective-permute-start | bytes 1253384 | tf_op jit(solution)/shard_map/xa1/ppermute | solution.py:52
  8.6 14.9 %collective-permute-start.1 = (bf16[272,768]{1,0:T(8,128)(2,1)}, bf16[272,768]{1,0:T(8,128)(2,1)S(1)}, u32[]{:S(2)}, u32[]{:S(2)}) collective-permute-start(bf16[272,768]{1,0:T(8,128)(2,1)} %get-tuple-element.32), channel_id=1, source_target_pairs={{0,246},{1,23},{2,240},{3,17},{4,242},{5,19},{6,244},{7,21},{8,254... | collective-permute-start | bytes 1253384 | tf_op jit(solution)/shard_map/xa3/ppermute | solution.py:52
  18.6 12.4 %collective-permute-start.8 = (bf16[272,768]{1,0:T(8,128)(2,1)}, bf16[272,768]{1,0:T(8,128)(2,1)S(1)}, u32[]{:S(2)}, u32[]{:S(2)}) collective-permute-start(bf16[272,768]{1,0:T(8,128)(2,1)} %get-tuple-element.44), channel_id=1, source_target_pairs={{0,9},{1,8},{2,11},{3,10},{4,13},{5,12},{6,15},{7,14},{8,1},{9,0},... | collective-permute-start | bytes 1253384 | tf_op jit(solution)/shard_map/sigma0/ppermute | solution.py:52
  18.7 1.0 %copy-start.1 = (bf16[256,768]{1,0:T(8,128)(2,1)S(1)}, bf16[256,768]{1,0:T(8,128)(2,1)}, u32[]{:S(2)}) copy-start(bf16[256,768]{1,0:T(8,128)(2,1)} %get-tuple-element.34.b) | copy-start | bytes 1179652
  19.7 3.9 %copy-start.2 = (f32[1,3072]{1,0:T(1,128)S(1)}, f32[1,3072]{1,0:T(1,128)}, u32[]{:S(2)}) copy-start(f32[1,3072]{1,0:T(1,128)} %gain.7) | copy-start | bytes 36868
  19.8 13.7 %collective-permute-start.9 = (bf16[256,768]{1,0:T(8,128)(2,1)S(1)}, bf16[256,768]{1,0:T(8,128)(2,1)S(1)}, u32[]{:S(2)}, u32[]{:S(2)}) collective-permute-start(bf16[256,768]{1,0:T(8,128)(2,1)S(1)} %get-tuple-element.35), channel_id=1, source_target_pairs={{0,8},{1,9},{2,10},{3,11},{4,12},{5,13},{6,14},{7,15},{8,0},{9,1},... | collective-permute-start | bytes 1179656 | tf_op jit(solution)/shard_map/tau2/ppermute | solution.py:52
  23.5 1.0 %copy-start.4 = (bf16[272,768]{1,0:T(8,128)(2,1)S(1)}, bf16[272,768]{1,0:T(8,128)(2,1)}, u32[]{:S(2)}) copy-start(bf16[272,768]{1,0:T(8,128)(2,1)} %get-tuple-element.36) | copy-start | bytes 1253380
  23.5 1.8 %copy-start.3 = (bf16[272,768]{1,0:T(8,128)(2,1)S(1)}, bf16[272,768]{1,0:T(8,128)(2,1)}, u32[]{:S(2)}) copy-start(bf16[272,768]{1,0:T(8,128)(2,1)} %get-tuple-element.39) | copy-start | bytes 1253380
  23.5 9.9 %copy-start = (bf16[272,768]{1,0:T(8,128)(2,1)S(1)}, bf16[272,768]{1,0:T(8,128)(2,1)}, u32[]{:S(2)}) copy-start(bf16[272,768]{1,0:T(8,128)(2,1)} %get-tuple-element.47.b.b0) | copy-start | bytes 1253380
  23.7 16.2 %collective-permute-start.4 = (bf16[272,768]{1,0:T(8,128)(2,1)S(1)}, bf16[272,768]{1,0:T(8,128)(2,1)S(1)}, u32[]{:S(2)}, u32[]{:S(2)}) collective-permute-start(bf16[272,768]{1,0:T(8,128)(2,1)S(1)} %mark.1), channel_id=1, source_target_pairs={{0,9},{1,8},{2,11},{3,10},{4,13},{5,12},{6,15},{7,14},{8,1},{9,0},... | collective-permute-start | bytes 1253384 | tf_op jit(solution)/shard_map/sigma1/ppermute | solution.py:52
  24.5 14.1 %collective-permute-start.3 = (bf16[272,768]{1,0:T(8,128)(2,1)S(1)}, bf16[272,768]{1,0:T(8,128)(2,1)S(1)}, u32[]{:S(2)}, u32[]{:S(2)}) collective-permute-start(bf16[272,768]{1,0:T(8,128)(2,1)S(1)} %copy-done.4), channel_id=1, source_target_pairs={{0,18},{1,243},{2,20},{3,245},{4,22},{5,247},{6,16},{7,241},{8,26}... | collective-permute-start | bytes 1253384 | tf_op jit(solution)/shard_map/xb1/ppermute | solution.py:52
  25.3 13.3 %collective-permute-start.5 = (bf16[272,768]{1,0:T(8,128)(2,1)S(1)}, bf16[272,768]{1,0:T(8,128)(2,1)S(1)}, u32[]{:S(2)}, u32[]{:S(2)}) collective-permute-start(bf16[272,768]{1,0:T(8,128)(2,1)S(1)} %copy-done.3), channel_id=1, source_target_pairs={{0,22},{1,247},{2,16},{3,241},{4,18},{5,243},{6,20},{7,245},{8,30}... | collective-permute-start | bytes 1253384 | tf_op jit(solution)/shard_map/xb3/ppermute | solution.py:52
  31.0 17.9 %collective-permute-start.12 = (bf16[272,768]{1,0:T(8,128)(2,1)S(1)}, bf16[272,768]{1,0:T(8,128)(2,1)S(1)}, u32[]{:S(2)}, u32[]{:S(2)}) collective-permute-start(bf16[272,768]{1,0:T(8,128)(2,1)S(1)} %collective-permute-done.1), channel_id=1, source_target_pairs={{0,9},{1,8},{2,11},{3,10},{4,13},{5,12},{6,15},{7,14},{8,1},{9,0},... | collective-permute-start | bytes 1253384 | tf_op jit(solution)/shard_map/sigma3/ppermute | solution.py:52
  33.5 11.7 %collective-permute-start.10 = (bf16[272,768]{1,0:T(8,128)(2,1)S(1)}, bf16[272,768]{1,0:T(8,128)(2,1)S(1)}, u32[]{:S(2)}, u32[]{:S(2)}) collective-permute-start(bf16[272,768]{1,0:T(8,128)(2,1)S(1)} %relay.6.own), channel_id=1, source_target_pairs={{0,8},{1,9},{2,10},{3,11},{4,12},{5,13},{6,14},{7,15},{8,0},{9,1},... | collective-permute-start | bytes 1253384 | tf_op jit(solution)/shard_map/tau0/ppermute | solution.py:52
  39.9 17.6 %collective-permute-start.7 = (bf16[256,768]{1,0:T(8,128)(2,1)S(1)}, bf16[256,768]{1,0:T(8,128)(2,1)S(1)}, u32[]{:S(2)}, u32[]{:S(2)}) collective-permute-start(bf16[256,768]{1,0:T(8,128)(2,1)S(1)} %get-tuple-element.43), channel_id=1, source_target_pairs={{0,20},{1,245},{2,22},{3,247},{4,16},{5,241},{6,18},{7,243},{8,28}... | collective-permute-start | bytes 1179656 | tf_op jit(solution)/shard_map/xk2/ppermute | solution.py:52
  40.0 14.1 %collective-permute-start.6 = (bf16[272,768]{1,0:T(8,128)(2,1)S(1)}, bf16[272,768]{1,0:T(8,128)(2,1)S(1)}, u32[]{:S(2)}, u32[]{:S(2)}) collective-permute-start(bf16[272,768]{1,0:T(8,128)(2,1)S(1)} %relay.5), channel_id=1, source_target_pairs={{0,8},{1,9},{2,10},{3,11},{4,12},{5,13},{6,14},{7,15},{8,0},{9,1},... | collective-permute-start | bytes 1253384 | tf_op jit(solution)/shard_map/tau1/ppermute | solution.py:52
  45.3 16.6 %collective-permute-start.11 = (bf16[272,768]{1,0:T(8,128)(2,1)S(1)}, bf16[272,768]{1,0:T(8,128)(2,1)S(1)}, u32[]{:S(2)}, u32[]{:S(2)}) collective-permute-start(bf16[272,768]{1,0:T(8,128)(2,1)S(1)} %get-tuple-element.48), channel_id=1, source_target_pairs={{0,20},{1,245},{2,22},{3,247},{4,16},{5,241},{6,18},{7,243},{8,28}... | collective-permute-start | bytes 1253384 | tf_op jit(solution)/shard_map/xt2/ppermute | solution.py:52
  45.4 17.9 %collective-permute-start.14 = (bf16[528,768]{1,0:T(8,128)(2,1)S(1)}, bf16[528,768]{1,0:T(8,128)(2,1)S(1)}, u32[]{:S(2)}, u32[]{:S(2)}) collective-permute-start(bf16[528,768]{1,0:T(8,128)(2,1)S(1)} %get-tuple-element.50), channel_id=1, source_target_pairs={{0,16},{1,241},{2,18},{3,243},{4,20},{5,245},{6,22},{7,247},{8,24}... | collective-permute-start | bytes 2433032 | tf_op jit(solution)/shard_map/both0/ppermute | solution.py:52
  48.9 14.4 %collective-permute-start.13 = (bf16[272,768]{1,0:T(8,128)(2,1)S(1)}, bf16[272,768]{1,0:T(8,128)(2,1)S(1)}, u32[]{:S(2)}, u32[]{:S(2)}) collective-permute-start(bf16[272,768]{1,0:T(8,128)(2,1)S(1)} %relay.7), channel_id=1, source_target_pairs={{0,8},{1,9},{2,10},{3,11},{4,12},{5,13},{6,14},{7,15},{8,0},{9,1},... | collective-permute-start | bytes 1253384 | tf_op jit(solution)/shard_map/tau3/ppermute | solution.py:52

commit v5 on v4

--- a/solution.py
+++ b/solution.py
@@ -101,18 +101,14 @@
         rows = pl.ds(part * step, step)
         return pltpu.make_async_copy(source.at[rows], hidden.at[rows], hidden_sems.at[part])
 
-    wait = cut_chunks(FIRST_CUTS, sources, held, in_sems)
     last = lax.axis_index("section") == SECTIONS - 1
     for edge, source in ((True, sources[0]), (False, sources[1])):
         @pl.when(last == edge)
         def _():
             for part in range(PARTS):
                 load(source, part).start()
+    wait = cut_chunks(FIRST_CUTS, sources, held, in_sems)
     stores = []
-    for r, chunk in enumerate(chunks):
-        wait(r)
-        stores.append(pltpu.make_async_copy(held.at[r], chunk.at[:ROWS], out_sems.at[r]))
-        stores[-1].start()
     sums = []
     for part in range(PARTS):
         load(sources[1], part).wait()
@@ -121,6 +117,13 @@
         power = jnp.sum(values * values, axis=1, keepdims=True)
         odd = lax.broadcasted_iota(jnp.int32, (step, 128), 1) % 2 == 1
         sums.append(jnp.where(odd, power, total))
+        if 1 <= part <= len(chunks):
+            wait(part - 1)
+            store = pltpu.make_async_copy(
+                held.at[part - 1], chunks[part - 1].at[:ROWS], out_sems.at[part - 1]
+            )
+            store.start()
+            stores.append(store)
     tail[...] = coded(jnp.concatenate(sums, axis=0).T[:EXTRA, :])
     for i, target in enumerate((chunks[1].at[ROWS:], chunks[2].at[ROWS:], tail_out)):
         stores.append(pltpu.make_async_copy(tail, target, tail_sems.at[i]))
@@ -325,7 +328,7 @@
     return hi, (a - hi.astype(jnp.float32)).astype(jnp.bfloat16)
 
 
-TILE = 256
+TILE, LANES = 256, 128
 STRIPES = [(slice(i, i + TILE), slice(0, i + TILE)) for i in range(0, BLK, TILE)]
 
 
@@ -345,15 +348,22 @@
 
 
 def invert(out, first, second, fourth, low_parts, low, whole, sems):
-    row = lax.broadcasted_iota(jnp.int32, (BLK, BLK), 0)
-    col = lax.broadcasted_iota(jnp.int32, (BLK, BLK), 1)
+    bound = jnp.max(jnp.sum(jnp.abs(whole[...]), axis=0, keepdims=True)) * (1.0 / TOKENS) + 0.05
+    inverse_bound = 1.0 / bound
+    row = lax.broadcasted_iota(jnp.int32, (LANES, LANES), 0)
+    col = lax.broadcasted_iota(jnp.int32, (LANES, LANES), 1)
     eye = jnp.where(row == col, 1.0, 0.0).astype(jnp.float32)
-    damped = whole[...] * (1.0 / TOKENS) + 0.05 * eye
-    bound = jnp.max(jnp.sum(jnp.abs(damped), axis=0, keepdims=True))
-    inverse_bound = 1.0 / bound
-    error = eye - damped * inverse_bound
-    first[0][...], first[1][...] = split(error)
-    low[...] = eye + error
+    for start in range(0, BLK, LANES):
+        end = start + LANES
+
+        def add_to_diagonal(block, amount):
+            pieces = [block[:, :start], block[:, start:end] + amount * eye, block[:, end:]]
+            return jnp.concatenate([piece for piece in pieces if piece.shape[1]], axis=1)
+
+        error = whole[start:end, :] * (inverse_bound * (-1.0 / TOKENS))
+        error = add_to_diagonal(error, 1.0 - 0.05 * inverse_bound)
+        first[0][start:end, :], first[1][start:end, :] = split(error)
+        low[start:end, :] = add_to_diagonal(error, 1.0)
     for rows, cols in STRIPES:
         value = product(first, first, rows, cols)
         put_symmetric(second, rows, cols, value, split)

time: 75.7 us -> 75.8 us (level)
  starting transfers between devices: 19 us -> 20.5 us
  waiting for transfers between devices: 32.8 us -> 31.7 us
    ppermute x15, starting transfers between devices: 19 us -> 20.5 us  [send(): return lax.ppermute(block, AXES, route)]
    ppermute x15, waiting for transfers between devices: 32.8 us -> 31.7 us  [send(): return lax.ppermute(block, AXES, route)]
where the time goes in v5:
time: 75.8 us; the launch traced here: 75.5 us
  waiting for transfers between devices  31.7 us (42%)
  Pallas kernels  21.1 us (28%)
  starting transfers between devices  20.5 us (27%)
  local copies, waits for them, and re-layouts  1.77 us (2%)
    ppermute x15, waiting for transfers between devices, send(): return lax.ppermute(block, AXES, route)  31.7 us
    ppermute x15, starting transfers between devices, send(): return lax.ppermute(block, AXES, route)  20.5 us
    pallas_call x3, Pallas kernels, in_vmem(): pl.pallas_call(kernel, out_shape=jax.ShapeDtypeStruct((BLK, BLK), jnp.flo...  14.6 us
    pallas_call x1, Pallas kernels, cut(): pl.pallas_call(second_cut_kernel, out_shape=[summed] * 4 + [plain], in_sp...  3.16 us
    pallas_call x1, Pallas kernels, cut(): pl.pallas_call(first_cut_kernel, out_shape=[plain, summed, summed, tail],...  2.86 us
    unnamed x10, local copies, waits for them, and re-layouts  1.77 us
  transfers between devices with their start and end apart: 15, of which 9 were waited for; matrix products, arithmetic and copies ran while one was open for 0% of the time, Pallas kernels for 8%

profile of v5, /device:TPU:1, one launch (start us, length us, event | category | flops | bytes accessed | tf_op | source)
XLA Modules:
  0.0 75.5 jit_solution(2701180642167403458)
XLA Ops:
  0.0 2.9 %cut1.1 = (bf16[256,768]{1,0:T(8,128)(2,1)}, bf16[272,768]{1,0:T(8,128)(2,1)}, bf16[272,768]{1,0:T(8,128)(2,1)}, bf16[16,768]{1,0:T(8,128)(2,1)}) custom-call(bf16[256,3072]{1,0:T(8,128)(2,1)} %refs_0_.3, bf16[256,3072]{1,0:T(8,128)(2,1)} %bitcast.3, bf16[256,3072]{1,0:T(8,128)(2,1)} %bitcast.5, bf16[256,3072]{1,0:T(8,128)(2,1)} %refs_3_.3), custom_call_target="tpu_custom_call" | custom-call | tf_op jit(solution)/shard_map/cut1/pallas_call | solution.py:157
  2.9 3.7 %collective-permute-start.2 = (bf16[256,768]{1,0:T(8,128)(2,1)}, bf16[256,768]{1,0:T(8,128)(2,1)S(1)}, u32[]{:S(2)}, u32[]{:S(2)}) collective-permute-start(bf16[256,768]{1,0:T(8,128)(2,1)} %get-tuple-element.33), channel_id=1, source_target_pairs={{0,9},{1,8},{2,11},{3,10},{4,13},{5,12},{6,15},{7,14},{8,1},{9,0},... | collective-permute-start | bytes 1179656 | tf_op jit(solution)/shard_map/sigma2/ppermute | solution.py:52
  6.5 2.1 %collective-permute-start = (bf16[272,768]{1,0:T(8,128)(2,1)}, bf16[272,768]{1,0:T(8,128)(2,1)S(1)}, u32[]{:S(2)}, u32[]{:S(2)}) collective-permute-start(bf16[272,768]{1,0:T(8,128)(2,1)} %get-tuple-element.31), channel_id=1, source_target_pairs={{0,242},{1,19},{2,244},{3,21},{4,246},{5,23},{6,240},{7,17},{8,250... | collective-permute-start | bytes 1253384 | tf_op jit(solution)/shard_map/xa1/ppermute | solution.py:52
  8.6 6.3 %collective-permute-start.1 = (bf16[272,768]{1,0:T(8,128)(2,1)}, bf16[272,768]{1,0:T(8,128)(2,1)S(1)}, u32[]{:S(2)}, u32[]{:S(2)}) collective-permute-start(bf16[272,768]{1,0:T(8,128)(2,1)} %get-tuple-element.32), channel_id=1, source_target_pairs={{0,246},{1,23},{2,240},{3,17},{4,242},{5,19},{6,244},{7,21},{8,254... | collective-permute-start | bytes 1253384 | tf_op jit(solution)/shard_map/xa3/ppermute | solution.py:52
  14.8 3.2 %cut2.1 = (bf16[272,768]{1,0:T(8,128)(2,1)}, bf16[272,768]{1,0:T(8,128)(2,1)}, bf16[272,768]{1,0:T(8,128)(2,1)}, bf16[272,768]{1,0:T(8,128)(2,1)}, bf16[256,768]{1,0:T(8,128)(2,1)}) custom-call(bf16[256,3072]{1,0:T(8,128)(2,1)} %refs_0_.3, bf16[256,3072]{1,0:T(8,128)(2,1)} %bitcast.4, bf16[256,3072]{1,0:T(8,128)(2,1)} %bitcast.6, bf16[256,3072]{1,0:T(8,128)(2,1)} %refs_3_.3, ...), custom_call_target="tpu_custom_call" | custom-call | tf_op jit(solution)/shard_map/cut2/pallas_call | solution.py:170
  18.1 1.0 %copy-done.1 = bf16[256,768]{1,0:T(8,128)(2,1)S(1)} copy-done((bf16[256,768]{1,0:T(8,128)(2,1)S(1)}, bf16[256,768]{1,0:T(8,128)(2,1)}, u32[]{:S(2)}) %copy-start.1) | copy-done | bytes 393240
  19.1 0.1 relay.4
  19.2 0.1 collective-permute-start.9
  19.3 4.2 %collective-permute-done.1 = bf16[272,768]{1,0:T(8,128)(2,1)S(1)} collective-permute-done((bf16[272,768]{1,0:T(8,128)(2,1)}, bf16[272,768]{1,0:T(8,128)(2,1)S(1)}, u32[]{:S(2)}, u32[]{:S(2)}) %collective-permute-start.1) | collective-permute-done | bytes 417824 | tf_op jit(solution)/shard_map/xa3/ppermute | solution.py:52
  23.5 0.1 mark.1
  23.6 0.1 collective-permute-start.4
  23.7 0.8 %copy-done.4 = bf16[272,768]{1,0:T(8,128)(2,1)S(1)} copy-done((bf16[272,768]{1,0:T(8,128)(2,1)S(1)}, bf16[272,768]{1,0:T(8,128)(2,1)}, u32[]{:S(2)}) %copy-start.4) | copy-done | bytes 417816
  24.5 0.8 collective-permute-start.3
  25.3 1.6 %collective-permute-start.5 = (bf16[272,768]{1,0:T(8,128)(2,1)S(1)}, bf16[272,768]{1,0:T(8,128)(2,1)S(1)}, u32[]{:S(2)}, u32[]{:S(2)}) collective-permute-start(bf16[272,768]{1,0:T(8,128)(2,1)S(1)} %copy-done.3), channel_id=1, source_target_pairs={{0,22},{1,247},{2,16},{3,241},{4,18},{5,243},{6,20},{7,245},{8,30}... | collective-permute-start | bytes 1253384 | tf_op jit(solution)/shard_map/xb3/ppermute | solution.py:52
  26.9 2.9 %collective-permute-done.8.a.a0 = bf16[272,768]{1,0:T(8,128)(2,1)S(1)} collective-permute-done((bf16[272,768]{1,0:T(8,128)(2,1)}, bf16[272,768]{1,0:T(8,128)(2,1)S(1)}, u32[]{:S(2)}, u32[]{:S(2)}) %collective-permute-start.8) | collective-permute-done | bytes 417824 | tf_op jit(solution)/shard_map/sigma0/ppermute | solution.py:52
  29.8 3.1 %collective-permute-start.12 = (bf16[272,768]{1,0:T(8,128)(2,1)S(1)}, bf16[272,768]{1,0:T(8,128)(2,1)S(1)}, u32[]{:S(2)}, u32[]{:S(2)}) collective-permute-start(bf16[272,768]{1,0:T(8,128)(2,1)S(1)} %collective-permute-done.1), channel_id=1, source_target_pairs={{0,9},{1,8},{2,11},{3,10},{4,13},{5,12},{6,15},{7,14},{8,1},{9,0},... | collective-permute-start | bytes 1253384 | tf_op jit(solution)/shard_map/sigma3/ppermute | solution.py:52
  32.9 0.1 collective-permute-start.10
  33.0 5.6 %collective-permute-done.3.b.b1 = bf16[272,768]{1,0:T(8,128)(2,1)S(1)} collective-permute-done((bf16[272,768]{1,0:T(8,128)(2,1)S(1)}, bf16[272,768]{1,0:T(8,128)(2,1)S(1)}, u32[]{:S(2)}, u32[]{:S(2)}) %collective-permute-start.3) | collective-permute-done | bytes 417824 | tf_op jit(solution)/shard_map/xb1/ppermute | solution.py:52
  38.6 0.1 collective-permute-done.4.a.a1
  38.7 1.2 %collective-permute-start.7 = (bf16[256,768]{1,0:T(8,128)(2,1)S(1)}, bf16[256,768]{1,0:T(8,128)(2,1)S(1)}, u32[]{:S(2)}, u32[]{:S(2)}) collective-permute-start(bf16[256,768]{1,0:T(8,128)(2,1)S(1)} %get-tuple-element.43), channel_id=1, source_target_pairs={{0,20},{1,245},{2,22},{3,247},{4,16},{5,241},{6,18},{7,243},{8,28}... | collective-permute-start | bytes 1179656 | tf_op jit(solution)/shard_map/xk2/ppermute | solution.py:52
  40.0 0.8 %collective-permute-start.6 = (bf16[272,768]{1,0:T(8,128)(2,1)S(1)}, bf16[272,768]{1,0:T(8,128)(2,1)S(1)}, u32[]{:S(2)}, u32[]{:S(2)}) collective-permute-start(bf16[272,768]{1,0:T(8,128)(2,1)S(1)} %relay.5), channel_id=1, source_target_pairs={{0,8},{1,9},{2,10},{3,11},{4,12},{5,13},{6,14},{7,15},{8,0},{9,1},... | collective-permute-start | bytes 1253384 | tf_op jit(solution)/shard_map/tau1/ppermute | solution.py:52
  40.8 3.3 %collective-permute-done.10.t0 = bf16[272,768]{1,0:T(8,128)(2,1)S(1)} collective-permute-done((bf16[272,768]{1,0:T(8,128)(2,1)S(1)}, bf16[272,768]{1,0:T(8,128)(2,1)S(1)}, u32[]{:S(2)}, u32[]{:S(2)}) %collective-permute-start.10) | collective-permute-done | bytes 417824 | tf_op jit(solution)/shard_map/tau0/ppermute | solution.py:52
  44.1 0.1 bundle.1
  44.3 0.4 collective-permute-start.14
  44.7 3.0 %collective-permute-done.12.a.a3 = bf16[272,768]{1,0:T(8,128)(2,1)S(1)} collective-permute-done((bf16[272,768]{1,0:T(8,128)(2,1)S(1)}, bf16[272,768]{1,0:T(8,128)(2,1)S(1)}, u32[]{:S(2)}, u32[]{:S(2)}) %collective-permute-start.12) | collective-permute-done | bytes 417824 | tf_op jit(solution)/shard_map/sigma3/ppermute | solution.py:52
  47.7 0.3 collective-permute-start.13
  48.0 4.9 %collective-permute-done.6.t1 = bf16[272,768]{1,0:T(8,128)(2,1)S(1)} collective-permute-done((bf16[272,768]{1,0:T(8,128)(2,1)S(1)}, bf16[272,768]{1,0:T(8,128)(2,1)S(1)}, u32[]{:S(2)}, u32[]{:S(2)}) %collective-permute-start.6) | collective-permute-done | bytes 417824 | tf_op jit(solution)/shard_map/tau1/ppermute | solution.py:52
  52.9 1.3 %early.1.acc = f32[768,768]{1,0:T(8,128)S(1)} custom-call(f32[1,3072]{1,0:T(1,128)S(1)} %copy-done.2, bf16[272,768]{1,0:T(8,128)(2,1)S(1)} %collective-permute-done.3.b.b1, bf16[272,768]{1,0:T(8,128)(2,1)S(1)} %collective-permute-done.4.a.a1, bf16[272,768]{1,0:T(8,128)(2,1)S(1)} %collective-permute-done.6.t1), custom_call_target="tpu_custom_call" | custom-call | flops 30000001024 | bytes 67108864 | tf_op jit(solution)/shard_map/early/pallas_call | solution.py:398
  54.3 3.2 %collective-permute-done.7.k2 = bf16[256,768]{1,0:T(8,128)(2,1)S(1)} collective-permute-done((bf16[256,768]{1,0:T(8,128)(2,1)S(1)}, bf16[256,768]{1,0:T(8,128)(2,1)S(1)}, u32[]{:S(2)}, u32[]{:S(2)}) %collective-permute-start.7) | collective-permute-done | bytes 393248 | tf_op jit(solution)/shard_map/xk2/ppermute | solution.py:52
  57.5 4.5 %collective-permute-done.11.t2 = bf16[272,768]{1,0:T(8,128)(2,1)S(1)} collective-permute-done((bf16[272,768]{1,0:T(8,128)(2,1)S(1)}, bf16[272,768]{1,0:T(8,128)(2,1)S(1)}, u32[]{:S(2)}, u32[]{:S(2)}) %collective-permute-start.11) | collective-permute-done | bytes 417824 | tf_op jit(solution)/shard_map/xt2/ppermute | solution.py:52
  62.0 1.3 %middle.1.acc = f32[768,768]{1,0:T(8,128)S(1)} custom-call(f32[768,768]{1,0:T(8,128)S(1)} %early.1.acc, f32[1,3072]{1,0:T(1,128)S(1)} %copy-done.2, bf16[272,768]{1,0:T(8,128)(2,1)S(1)} %collective-permute-done.4.a.a1, bf16[256,768]{1,0:T(8,128)(2,1)S(1)} %collective-permute-done.7.k2, bf16[272,768]{1,0:T(8,128)(2,1)S(1)} %collective-permute-done.11.t2), custom_call_target="tpu_custom_call" | custom-call | flops 30000001024 | bytes 67108864 | tf_op jit(solution)/shard_map/middle/pallas_call | solution.py:398
  63.3 12.0 %last.1 = f32[768,768]{1,0:T(8,128)} custom-call(f32[768,768]{1,0:T(8,128)S(1)} %middle.1.acc, f32[1,3072]{1,0:T(1,128)S(1)} %copy-done.2, bf16[272,768]{1,0:T(8,128)(2,1)S(1)} %collective-permute-done.4.a.a1, bf16[272,768]{1,0:T(8,128)(2,1)S(1)} %collective-permute-done.5.b.b3, bf16[272,768]{1,0:T(8,128)(2,1)S(1)} %collective-permute-done.12.a.a3, ...), custom_call_target="tpu_custom_call" | custom-call | flops 30000001024 | bytes 67108864 | tf_op jit(solution)/shard_map/last/pallas_call | solution.py:398
  (19 shorter events, 0.4 us)
Async XLA Ops:
  2.9 15.2 %collective-permute-start.2 = (bf16[256,768]{1,0:T(8,128)(2,1)}, bf16[256,768]{1,0:T(8,128)(2,1)S(1)}, u32[]{:S(2)}, u32[]{:S(2)}) collective-permute-start(bf16[256,768]{1,0:T(8,128)(2,1)} %get-tuple-element.33), channel_id=1, source_target_pairs={{0,9},{1,8},{2,11},{3,10},{4,13},{5,12},{6,15},{7,14},{8,1},{9,0},... | collective-permute-start | bytes 1179656 | tf_op jit(solution)/shard_map/sigma2/ppermute | solution.py:52
  6.5 12.8 %collective-permute-start = (bf16[272,768]{1,0:T(8,128)(2,1)}, bf16[272,768]{1,0:T(8,128)(2,1)S(1)}, u32[]{:S(2)}, u32[]{:S(2)}) collective-permute-start(bf16[272,768]{1,0:T(8,128)(2,1)} %get-tuple-element.31), channel_id=1, source_target_pairs={{0,242},{1,19},{2,244},{3,21},{4,246},{5,23},{6,240},{7,17},{8,250... | collective-permute-start | bytes 1253384 | tf_op jit(solution)/shard_map/xa1/ppermute | solution.py:52
  8.6 14.9 %collective-permute-start.1 = (bf16[272,768]{1,0:T(8,128)(2,1)}, bf16[272,768]{1,0:T(8,128)(2,1)S(1)}, u32[]{:S(2)}, u32[]{:S(2)}) collective-permute-start(bf16[272,768]{1,0:T(8,128)(2,1)} %get-tuple-element.32), channel_id=1, source_target_pairs={{0,246},{1,23},{2,240},{3,17},{4,242},{5,19},{6,244},{7,21},{8,254... | collective-permute-start | bytes 1253384 | tf_op jit(solution)/shard_map/xa3/ppermute | solution.py:52
  18.0 11.8 %collective-permute-start.8 = (bf16[272,768]{1,0:T(8,128)(2,1)}, bf16[272,768]{1,0:T(8,128)(2,1)S(1)}, u32[]{:S(2)}, u32[]{:S(2)}) collective-permute-start(bf16[272,768]{1,0:T(8,128)(2,1)} %get-tuple-element.44), channel_id=1, source_target_pairs={{0,9},{1,8},{2,11},{3,10},{4,13},{5,12},{6,15},{7,14},{8,1},{9,0},... | collective-permute-start | bytes 1253384 | tf_op jit(solution)/shard_map/sigma0/ppermute | solution.py:52
  18.1 1.0 %copy-start.1 = (bf16[256,768]{1,0:T(8,128)(2,1)S(1)}, bf16[256,768]{1,0:T(8,128)(2,1)}, u32[]{:S(2)}) copy-start(bf16[256,768]{1,0:T(8,128)(2,1)} %get-tuple-element.34.b) | copy-start | bytes 1179652
  19.1 4.4 %copy-start.2 = (f32[1,3072]{1,0:T(1,128)S(1)}, f32[1,3072]{1,0:T(1,128)}, u32[]{:S(2)}) copy-start(f32[1,3072]{1,0:T(1,128)} %gain.7) | copy-start | bytes 36868
  19.2 13.6 %collective-permute-start.9 = (bf16[256,768]{1,0:T(8,128)(2,1)S(1)}, bf16[256,768]{1,0:T(8,128)(2,1)S(1)}, u32[]{:S(2)}, u32[]{:S(2)}) collective-permute-start(bf16[256,768]{1,0:T(8,128)(2,1)S(1)} %get-tuple-element.35), channel_id=1, source_target_pairs={{0,8},{1,9},{2,10},{3,11},{4,12},{5,13},{6,14},{7,15},{8,0},{9,1},... | collective-permute-start | bytes 1179656 | tf_op jit(solution)/shard_map/tau2/ppermute | solution.py:52
  23.5 1.0 %copy-start.4 = (bf16[272,768]{1,0:T(8,128)(2,1)S(1)}, bf16[272,768]{1,0:T(8,128)(2,1)}, u32[]{:S(2)}) copy-start(bf16[272,768]{1,0:T(8,128)(2,1)} %get-tuple-element.36) | copy-start | bytes 1253380
  23.5 1.8 %copy-start.3 = (bf16[272,768]{1,0:T(8,128)(2,1)S(1)}, bf16[272,768]{1,0:T(8,128)(2,1)}, u32[]{:S(2)}) copy-start(bf16[272,768]{1,0:T(8,128)(2,1)} %get-tuple-element.39) | copy-start | bytes 1253380
  23.5 9.3 %copy-start = (bf16[272,768]{1,0:T(8,128)(2,1)S(1)}, bf16[272,768]{1,0:T(8,128)(2,1)}, u32[]{:S(2)}) copy-start(bf16[272,768]{1,0:T(8,128)(2,1)} %get-tuple-element.47.b.b0) | copy-start | bytes 1253380
  23.6 15.1 %collective-permute-start.4 = (bf16[272,768]{1,0:T(8,128)(2,1)S(1)}, bf16[272,768]{1,0:T(8,128)(2,1)S(1)}, u32[]{:S(2)}, u32[]{:S(2)}) collective-permute-start(bf16[272,768]{1,0:T(8,128)(2,1)S(1)} %mark.1), channel_id=1, source_target_pairs={{0,9},{1,8},{2,11},{3,10},{4,13},{5,12},{6,15},{7,14},{8,1},{9,0},... | collective-permute-start | bytes 1253384 | tf_op jit(solution)/shard_map/sigma1/ppermute | solution.py:52
  24.5 14.1 %collective-permute-start.3 = (bf16[272,768]{1,0:T(8,128)(2,1)S(1)}, bf16[272,768]{1,0:T(8,128)(2,1)S(1)}, u32[]{:S(2)}, u32[]{:S(2)}) collective-permute-start(bf16[272,768]{1,0:T(8,128)(2,1)S(1)} %copy-done.4), channel_id=1, source_target_pairs={{0,18},{1,243},{2,20},{3,245},{4,22},{5,247},{6,16},{7,241},{8,26}... | collective-permute-start | bytes 1253384 | tf_op jit(solution)/shard_map/xb1/ppermute | solution.py:52
  25.3 13.3 %collective-permute-start.5 = (bf16[272,768]{1,0:T(8,128)(2,1)S(1)}, bf16[272,768]{1,0:T(8,128)(2,1)S(1)}, u32[]{:S(2)}, u32[]{:S(2)}) collective-permute-start(bf16[272,768]{1,0:T(8,128)(2,1)S(1)} %copy-done.3), channel_id=1, source_target_pairs={{0,22},{1,247},{2,16},{3,241},{4,18},{5,243},{6,20},{7,245},{8,30}... | collective-permute-start | bytes 1253384 | tf_op jit(solution)/shard_map/xb3/ppermute | solution.py:52
  29.8 17.9 %collective-permute-start.12 = (bf16[272,768]{1,0:T(8,128)(2,1)S(1)}, bf16[272,768]{1,0:T(8,128)(2,1)S(1)}, u32[]{:S(2)}, u32[]{:S(2)}) collective-permute-start(bf16[272,768]{1,0:T(8,128)(2,1)S(1)} %collective-permute-done.1), channel_id=1, source_target_pairs={{0,9},{1,8},{2,11},{3,10},{4,13},{5,12},{6,15},{7,14},{8,1},{9,0},... | collective-permute-start | bytes 1253384 | tf_op jit(solution)/shard_map/sigma3/ppermute | solution.py:52
  32.9 11.2 %collective-permute-start.10 = (bf16[272,768]{1,0:T(8,128)(2,1)S(1)}, bf16[272,768]{1,0:T(8,128)(2,1)S(1)}, u32[]{:S(2)}, u32[]{:S(2)}) collective-permute-start(bf16[272,768]{1,0:T(8,128)(2,1)S(1)} %relay.6.own), channel_id=1, source_target_pairs={{0,8},{1,9},{2,10},{3,11},{4,12},{5,13},{6,14},{7,15},{8,0},{9,1},... | collective-permute-start | bytes 1253384 | tf_op jit(solution)/shard_map/tau0/ppermute | solution.py:52
  38.7 18.8 %collective-permute-start.7 = (bf16[256,768]{1,0:T(8,128)(2,1)S(1)}, bf16[256,768]{1,0:T(8,128)(2,1)S(1)}, u32[]{:S(2)}, u32[]{:S(2)}) collective-permute-start(bf16[256,768]{1,0:T(8,128)(2,1)S(1)} %get-tuple-element.43), channel_id=1, source_target_pairs={{0,20},{1,245},{2,22},{3,247},{4,16},{5,241},{6,18},{7,243},{8,28}... | collective-permute-start | bytes 1179656 | tf_op jit(solution)/shard_map/xk2/ppermute | solution.py:52
  40.0 12.9 %collective-permute-start.6 = (bf16[272,768]{1,0:T(8,128)(2,1)S(1)}, bf16[272,768]{1,0:T(8,128)(2,1)S(1)}, u32[]{:S(2)}, u32[]{:S(2)}) collective-permute-start(bf16[272,768]{1,0:T(8,128)(2,1)S(1)} %relay.5), channel_id=1, source_target_pairs={{0,8},{1,9},{2,10},{3,11},{4,12},{5,13},{6,14},{7,15},{8,0},{9,1},... | collective-permute-start | bytes 1253384 | tf_op jit(solution)/shard_map/tau1/ppermute | solution.py:52
  44.2 17.8 %collective-permute-start.11 = (bf16[272,768]{1,0:T(8,128)(2,1)S(1)}, bf16[272,768]{1,0:T(8,128)(2,1)S(1)}, u32[]{:S(2)}, u32[]{:S(2)}) collective-permute-start(bf16[272,768]{1,0:T(8,128)(2,1)S(1)} %get-tuple-element.48), channel_id=1, source_target_pairs={{0,20},{1,245},{2,22},{3,247},{4,16},{5,241},{6,18},{7,243},{8,28}... | collective-permute-start | bytes 1253384 | tf_op jit(solution)/shard_map/xt2/ppermute | solution.py:52
  44.3 19.1 %collective-permute-start.14 = (bf16[528,768]{1,0:T(8,128)(2,1)S(1)}, bf16[528,768]{1,0:T(8,128)(2,1)S(1)}, u32[]{:S(2)}, u32[]{:S(2)}) collective-permute-start(bf16[528,768]{1,0:T(8,128)(2,1)S(1)} %get-tuple-element.50), channel_id=1, source_target_pairs={{0,16},{1,241},{2,18},{3,243},{4,20},{5,245},{6,22},{7,247},{8,24}... | collective-permute-start | bytes 2433032 | tf_op jit(solution)/shard_map/both0/ppermute | solution.py:52
  47.7 15.6 %collective-permute-start.13 = (bf16[272,768]{1,0:T(8,128)(2,1)S(1)}, bf16[272,768]{1,0:T(8,128)(2,1)S(1)}, u32[]{:S(2)}, u32[]{:S(2)}) collective-permute-start(bf16[272,768]{1,0:T(8,128)(2,1)S(1)} %relay.7), channel_id=1, source_target_pairs={{0,8},{1,9},{2,10},{3,11},{4,12},{5,13},{6,14},{7,15},{8,0},{9,1},... | collective-permute-start | bytes 1253384 | tf_op jit(solution)/shard_map/tau3/ppermute | solution.py:52
